TPU v7x, 32 devices: a whole 2x2x4 slice. The times are simulated.
32 devices in a mesh: groups: 2 (over y), space: 16 (over z, x, core).
Axes of the slice: x: 2, y: 2, z: 4, core: 2. Of those that a mesh axis runs over, the one named last changes fastest.
Arguments:
- field: bfloat16 [32, 96, 96, 128], P(('groups', 'space')), parts along dimension 0, may hold values from -6 to 6
- cotangent: bfloat16 [32, 96, 96, 128], P(('groups', 'space')), parts along dimension 0, may hold values from -6 to 6
- spectral_weight: bfloat16 [4608, 24, 128], P('space'), may hold values from -6 to 6
- skip_weight: bfloat16 [8, 8], replicated, may hold values from -2 to 2
- bias: bfloat16 [8], replicated, may hold values from -3 to 3
Outputs:
- output: bfloat16 [32, 96, 96, 128], P(('groups', 'space')), parts along dimension 0
- field_grad: bfloat16 [32, 96, 96, 128], P(('groups', 'space')), parts along dimension 0
- spectral_grad: float32 [9216, 24, 128], P(('groups', 'space')), parts along dimension 0
- skip_grad: float32 [16, 8], P('groups'), parts along dimension 0
- bias_grad: float32 [16], P('groups'), parts along dimension 0
There are 2 independent parts, one for each index of `groups`. A program takes and returns all parts, laid end to end along the dimension named above; an argument that names none is the same for every part. Nothing has to cross between parts.
All inputs are finite; a program needn't handle non-finite values.
Results may differ from a plain program's by a relative error of at most 0.008.
Values sent between devices are 32-bit elements; how exact they have to be, the bound alone decides.
A program may use at most 128 MiB of HBM per device.

v0:
```python
import functools
import math

import jax
import jax.numpy as jnp
import ml_dtypes
import numpy as np
from jax import lax
from jax.experimental import pallas as pl
from jax.experimental.pallas import tpu as pltpu
from jax.sharding import PartitionSpec as P

KX = 24
KY = 24
KZ = 24
KT = 8


FULL_PRECISION = lax.Precision.HIGHEST


def angle_pair(freqs, positions, length):
    product = freqs[:, None] * positions[None, :] % length
    angles = product.astype(jnp.float32) * (2.0 * math.pi / length)
    return (jnp.cos(angles), jnp.sin(angles))


def centred(count):
    return jnp.arange(count, dtype=jnp.int32) - count // 2


def kron_eye(base, channels):
    eye_matrix = jnp.eye(channels, dtype=jnp.float32)
    rows_in, cols_in = base.shape
    return (base[:, None, :, None] * eye_matrix[None, :, None, :]).reshape(
        rows_in * channels, cols_in * channels
    )


def block_diagonal(weight, copies):
    eye_matrix = jnp.eye(copies, dtype=jnp.float32)
    width_in, width_out = weight.shape
    return (eye_matrix[:, None, :, None] * weight[None, :, None, :]).reshape(
        copies * width_in, copies * width_out
    )


def turned_forward(values):
    half = values.shape[-1] // 2
    return jnp.concatenate([values[..., half:], -values[..., :half]], axis=-1)


def turned_back(values):
    half = values.shape[-1] // 2
    return jnp.concatenate([-values[..., half:], values[..., :half]], axis=-1)


def plane_spectra(values, time_table, channels):
    cells_x, rows_y, rows_z, _ = values.shape
    mixed_t = jnp.dot(values, time_table, preferred_element_type=jnp.float32)
    cosine_z, sine_z = angle_pair(centred(KZ), jnp.arange(rows_z, dtype=jnp.int32), rows_z)
    table_z = jnp.concatenate([cosine_z, sine_z], axis=1)
    stacked_z = jnp.concatenate([mixed_t, turned_forward(mixed_t)], axis=2)
    along_z = jnp.einsum("kz,xyzm->xykm", table_z, stacked_z, precision=FULL_PRECISION)
    cosine_y, sine_y = angle_pair(centred(KY), jnp.arange(rows_y, dtype=jnp.int32), rows_y)
    table_y = jnp.concatenate([cosine_y, sine_y], axis=1)
    stacked_y = jnp.concatenate([along_z, turned_forward(along_z)], axis=1)
    along_y = jnp.einsum("jy,xykm->xjkm", table_y, stacked_y, precision=FULL_PRECISION)
    grid = along_y.reshape(cells_x, KY, KZ, 2, KT, channels).transpose(0, 1, 2, 4, 3, 5)
    return grid.reshape(cells_x, KY * KZ * KT, 2 * channels)


def plane_fields(planes, inverse_table, rows_y, rows_z):
    cells_x = planes.shape[0]
    channels = planes.shape[2] // 2
    grid = planes.reshape(cells_x, KY, KZ, KT, 2, channels).transpose(0, 1, 2, 4, 3, 5)
    grid = grid.reshape(cells_x, KY, KZ, 2 * KT * channels)
    cosine_y, sine_y = angle_pair(centred(KY), jnp.arange(rows_y, dtype=jnp.int32), rows_y)
    table_y = jnp.concatenate([cosine_y.T, sine_y.T], axis=1)
    stacked_y = jnp.concatenate([grid, turned_back(grid)], axis=1)
    along_y = jnp.einsum("yj,xjkm->xykm", table_y, stacked_y, precision=FULL_PRECISION)
    timed = jnp.dot(
        along_y, inverse_table, precision=FULL_PRECISION, preferred_element_type=jnp.float32
    )
    width_out = timed.shape[3] // 2
    cosine_z, sine_z = angle_pair(centred(KZ), jnp.arange(rows_z, dtype=jnp.int32), rows_z)
    table_z = jnp.stack([cosine_z.T, -sine_z.T], axis=2).reshape(rows_z, 2 * KZ)
    paired = timed.reshape(cells_x, rows_y, 2 * KZ, width_out)
    return jnp.einsum("zk,xykm->xyzm", table_z, paired, precision=FULL_PRECISION)


def along_x(planes, positions, length):
    channels = planes.shape[2] // 2
    cosine_x, sine_x = angle_pair(centred(KX), positions, length)
    real_part = planes[..., :channels]
    imag_part = planes[..., channels:]
    real_k = jnp.einsum("kx,xmc->mkc", cosine_x, real_part, precision=FULL_PRECISION) + jnp.einsum(
        "kx,xmc->mkc", sine_x, imag_part, precision=FULL_PRECISION
    )
    imag_k = jnp.einsum("kx,xmc->mkc", cosine_x, imag_part, precision=FULL_PRECISION) - jnp.einsum(
        "kx,xmc->mkc", sine_x, real_part, precision=FULL_PRECISION
    )
    return jnp.concatenate([real_k, imag_k], axis=2)


def back_along_x(spectra, positions, length):
    channels = spectra.shape[2] // 2
    cosine_x, sine_x = angle_pair(centred(KX), positions, length)
    real_part = spectra[..., :channels]
    imag_part = spectra[..., channels:]
    real_x = jnp.einsum("kx,mkc->xmc", cosine_x, real_part, precision=FULL_PRECISION) - jnp.einsum(
        "kx,mkc->xmc", sine_x, imag_part, precision=FULL_PRECISION
    )
    imag_x = jnp.einsum("kx,mkc->xmc", cosine_x, imag_part, precision=FULL_PRECISION) + jnp.einsum(
        "kx,mkc->xmc", sine_x, real_part, precision=FULL_PRECISION
    )
    return jnp.concatenate([real_x, imag_x], axis=2)


def split_weight(weights, channels):
    modes, freqs, _ = weights.shape
    shaped = weights.reshape(modes, freqs, 2, channels, channels)
    return (shaped[:, :, 0], shaped[:, :, 1])


def mix_forward(spectra, weights):
    channels = spectra.shape[2] // 2
    weight_real, weight_imag = split_weight(weights, channels)
    real_part = spectra[..., :channels]
    imag_part = spectra[..., channels:]
    out_real = jnp.einsum(
        "mki,mkio->mko", real_part, weight_real, precision=FULL_PRECISION
    ) - jnp.einsum("mki,mkio->mko", imag_part, weight_imag, precision=FULL_PRECISION)
    out_imag = jnp.einsum(
        "mki,mkio->mko", real_part, weight_imag, precision=FULL_PRECISION
    ) + jnp.einsum("mki,mkio->mko", imag_part, weight_real, precision=FULL_PRECISION)
    return jnp.concatenate([out_real, out_imag], axis=2)


def mix_adjoint(spectra, weights):
    channels = spectra.shape[2] // 2
    weight_real, weight_imag = split_weight(weights, channels)
    real_part = spectra[..., :channels]
    imag_part = spectra[..., channels:]
    out_real = jnp.einsum(
        "mko,mkio->mki", real_part, weight_real, precision=FULL_PRECISION
    ) + jnp.einsum("mko,mkio->mki", imag_part, weight_imag, precision=FULL_PRECISION)
    out_imag = jnp.einsum(
        "mko,mkio->mki", imag_part, weight_real, precision=FULL_PRECISION
    ) - jnp.einsum("mko,mkio->mki", real_part, weight_imag, precision=FULL_PRECISION)
    return jnp.concatenate([out_real, out_imag], axis=2)


def weight_gradient(source, target):
    modes, freqs, double = source.shape
    channels = double // 2
    src_real = source[..., :channels]
    src_imag = source[..., channels:]
    tgt_real = target[..., :channels]
    tgt_imag = target[..., channels:]
    real_w = jnp.einsum("mki,mko->mkio", src_real, tgt_real, precision=FULL_PRECISION) + jnp.einsum(
        "mki,mko->mkio", src_imag, tgt_imag, precision=FULL_PRECISION
    )
    imag_w = jnp.einsum("mki,mko->mkio", src_real, tgt_imag, precision=FULL_PRECISION) - jnp.einsum(
        "mki,mko->mkio", src_imag, tgt_real, precision=FULL_PRECISION
    )
    return jnp.stack([real_w, imag_w], axis=2).reshape(modes, freqs, 2 * channels * channels)


def gelu_slope(values):
    normal_cdf = 0.5 * (1.0 + jax.scipy.special.erf(values * (1.0 / math.sqrt(2.0))))
    normal_pdf = jnp.exp(-0.5 * values * values) * (1.0 / math.sqrt(2.0 * math.pi))
    return normal_cdf + values * normal_pdf


def on_device(field, cotangent, spectral_weight, skip_weight, bias):
    cells_x, rows_y, rows_z, last_dim = field.shape
    channels = skip_weight.shape[0]
    steps_t = last_dim // channels
    devices = lax.axis_size("space")
    length_x = cells_x * devices
    total = length_x * rows_y * rows_z * steps_t
    every_x = jnp.arange(length_x, dtype=jnp.int32)
    cosine_t, sine_t = angle_pair(
        jnp.arange(KT, dtype=jnp.int32), jnp.arange(steps_t, dtype=jnp.int32), steps_t
    )
    forward_base = jnp.stack([cosine_t.T, -sine_t.T], axis=1).reshape(steps_t, 2 * KT)
    time_table = kron_eye(forward_base, channels).astype(jnp.bfloat16)
    upper_rows = jnp.concatenate([cosine_t, sine_t], axis=1)
    lower_rows = jnp.concatenate([-sine_t, cosine_t], axis=1)
    inverse_base = jnp.concatenate([upper_rows, lower_rows], axis=0) / total
    inverse_table = kron_eye(inverse_base, channels)
    weight_f32 = spectral_weight.astype(jnp.float32)
    skip_f32 = skip_weight.astype(jnp.float32)

    def to_owner(planes):
        arrived = lax.all_to_all(planes, "space", split_axis=1, concat_axis=0, tiled=True)
        return along_x(arrived, every_x, length_x)

    def to_planes(spectra):
        columns = back_along_x(spectra, every_x, length_x)
        return lax.all_to_all(columns, "space", split_axis=0, concat_axis=1, tiled=True)

    own_field = to_owner(plane_spectra(field, time_table, channels))
    skip_table = block_diagonal(skip_f32, steps_t).astype(jnp.bfloat16)
    skip_part = jnp.dot(field, skip_table, preferred_element_type=jnp.float32)
    spectral_part = plane_fields(
        to_planes(mix_forward(own_field, weight_f32)), inverse_table, rows_y, rows_z
    )
    pre_act = spectral_part + skip_part + jnp.tile(bias.astype(jnp.float32), steps_t)
    output = jax.nn.gelu(pre_act, approximate=False).astype(jnp.bfloat16)
    grad_pre = (cotangent.astype(jnp.float32) * gelu_slope(pre_act)).astype(jnp.bfloat16)
    own_grad = to_owner(plane_spectra(grad_pre, time_table, channels))
    skip_back = block_diagonal(skip_f32.T, steps_t).astype(jnp.bfloat16)
    local_back = jnp.dot(grad_pre, skip_back, preferred_element_type=jnp.float32)
    flat_field = field.reshape(-1, last_dim)
    flat_grad = grad_pre.reshape(-1, last_dim)
    outer_sum = lax.dot_general(
        flat_field, flat_grad, (((0,), (0,)), ((), ())), preferred_element_type=jnp.float32
    )
    local_skip = jnp.einsum("tatb->ab", outer_sum.reshape(steps_t, channels, steps_t, channels))
    local_bias = jnp.sum(flat_grad.reshape(-1, steps_t, channels), axis=(0, 1), dtype=jnp.float32)
    skip_total, bias_total = lax.psum((local_skip, local_bias), "space")
    spectral_grad = weight_gradient(own_field, own_grad / total)
    back_part = plane_fields(
        to_planes(mix_adjoint(own_grad, weight_f32)), inverse_table, rows_y, rows_z
    )
    field_grad = (back_part + local_back).astype(jnp.bfloat16)
    scale = 1.0 / math.sqrt(total)
    return (output, field_grad, spectral_grad, skip_total * scale, bias_total * scale)


PAD_ROWS = 8


def split_pair(values):
    high = values.astype(jnp.bfloat16)
    low = (values - high.astype(jnp.float32)).astype(jnp.bfloat16)
    return high, low


def dot32(left, right):
    return jnp.dot(left, right, preferred_element_type=jnp.float32)


def np_angles(freqs, positions, length):
    angles = (np.outer(freqs, positions) % length) * (2.0 * math.pi / length)
    return np.cos(angles), np.sin(angles)


def np_split(table):
    high = table.astype(np.float32).astype(ml_dtypes.bfloat16)
    low = (table - high.astype(np.float64)).astype(np.float32).astype(ml_dtypes.bfloat16)
    return high, low


def np_bf16(table):
    return table.astype(np.float32).astype(ml_dtypes.bfloat16)


def make_tables(rows_y, rows_z, steps_t, channels, devices):
    half = KT * channels
    lanes = 2 * half
    eye_c = np.eye(channels)
    cos_z, sin_z = np_angles(np.arange(KZ) - KZ // 2, np.arange(rows_z), rows_z)
    cos_y, sin_y = np_angles(np.arange(KY) - KY // 2, np.arange(rows_y), rows_y)
    cos_t, sin_t = np_angles(np.arange(KT), np.arange(steps_t), steps_t)
    cos_x, sin_x = np_angles(np.arange(KX) - KX // 2, np.arange(devices), devices)
    tables = {}
    tables["z_fwd"] = np_bf16(np.concatenate([cos_z, sin_z], 0))
    tables["y_fwd"] = np_bf16(np.concatenate([cos_y, sin_y], 0))
    time_fwd = np.kron(np.stack([cos_t.T, -sin_t.T], 1).reshape(steps_t, 2 * KT), eye_c)
    turned = np.concatenate([time_fwd[:, half:], -time_fwd[:, :half]], 1)
    tables["t_fwd"] = np_bf16(np.concatenate([time_fwd, turned], 0))
    y_high, y_low = np_split(np.concatenate([cos_y.T, sin_y.T], 1))
    tables["y_back"] = np.concatenate([y_high, y_high, y_low], 1)
    time_back = np.concatenate(
        [np.concatenate([cos_t, sin_t], 1), np.concatenate([-sin_t, cos_t], 1)], 0
    )
    tables["t_back"] = np_bf16(np.kron(time_back, eye_c))
    tables["z_back"] = np_bf16(np.concatenate([cos_z.T, -sin_z.T], 1))
    eye_p = np.eye(PAD_ROWS)

    def spread(base):
        return np.einsum("kx,pq->pkxq", base, eye_p).reshape(
            PAD_ROWS * KX, devices * PAD_ROWS
        )

    x_high, x_low = np_split(np.concatenate([spread(cos_x), spread(sin_x)], 0))
    tables["x_fwd"] = np.concatenate([x_high, x_high, x_low], 1)
    tables["x_back"] = np.concatenate(
        np_split(np.concatenate([spread(cos_x).T, spread(sin_x).T], 1)), 0
    )
    c = channels
    pick_s = np.zeros((KT, 2, KT, c, 2, 2, c, c))
    pick_t = np.zeros((KT, 2, KT, c, 2, 2, c, c))
    fold_s = np.zeros((KT, 2, 2, c, c, 2, KT, c))
    fold_t = np.zeros((KT, 2, 2, c, c, 2, KT, c))
    for k in range(KT):
        for a in range(c):
            pick_s[k, 0, k, a, 0, :, a, :] = 1
            pick_s[k, 1, k, a, 1, 0, a, :] = 1
            pick_s[k, 1, k, a, 1, 1, a, :] = -1
            pick_t[k, 0, k, a, 0, 0, :, a] = 1
            pick_t[k, 1, k, a, 0, 1, :, a] = 1
            pick_t[k, 1, k, a, 1, 0, :, a] = 1
            pick_t[k, 0, k, a, 1, 1, :, a] = 1
            fold_s[k, 0, 0, :, a, 0, k, a] = 1
            fold_s[k, 1, 1, :, a, 0, k, a] = 1
            fold_s[k, 0, 1, :, a, 1, k, a] = 1
            fold_s[k, 1, 0, :, a, 1, k, a] = 1
            fold_t[k, 0, :, a, :, 0, k, a] = 1
            fold_t[k, 1, 0, a, :, 1, k, a] = 1
            fold_t[k, 1, 1, a, :, 1, k, a] = -1
    wide = 2 * c * c

    def doubled(pick):
        flat = pick.reshape(KT, lanes, 2 * wide)
        return np_bf16(np.concatenate([flat, flat], 1))

    tables["pick_s"] = doubled(pick_s)
    tables["pick_t"] = doubled(pick_t)
    tables["fold_s"] = np_bf16(fold_s.reshape(KT, 2 * wide, lanes))
    tables["fold_t"] = np_bf16(fold_t.reshape(KT, 2 * wide, lanes))
    return {name: jnp.asarray(table) for name, table in tables.items()}


def half_sign(shape, first, second):
    lane = lax.broadcasted_iota(jnp.int32, shape, 1)
    return jnp.where(lane < shape[1] // 2, first, second).astype(jnp.float32)


def roll_half(values):
    return pltpu.roll(values, values.shape[1] // 2, 1)


def z_forward(rows, count, z_table, t_table):
    pieces = []
    for y in range(count):
        both = dot32(z_table, rows(y))
        pieces.append(jnp.concatenate([both[:KZ], both[KZ:]], axis=1))
    stacked = jnp.concatenate(pieces, axis=0).astype(jnp.bfloat16)
    return dot32(stacked, t_table)


def y_forward(zbuf, spec, y_table, rows_y, lanes):
    sign = half_sign((KY, lanes), 1.0, -1.0)
    for kz in range(KZ):
        column = zbuf[pl.ds(kz, rows_y, stride=KZ), :].astype(jnp.bfloat16)
        both = dot32(y_table, column)
        spec[pl.ds(kz, KY, stride=KZ), :] = both[:KY] + sign * roll_half(both[KY:])


def y_backward(spec, ubuf, y_table, rows_y, lanes):
    sign = half_sign((KY, lanes), -1.0, 1.0)
    for kz in range(KZ):
        column = spec[pl.ds(kz, KY, stride=KZ), :]
        both = jnp.concatenate([column, sign * roll_half(column)], axis=0)
        high, low = split_pair(both)
        stacked = jnp.concatenate([high, low, high], axis=0)
        ubuf[pl.ds(kz, rows_y, stride=KZ), :] = dot32(y_table, stacked)


def z_backward(ubuf, start, count, t_table):
    lanes = ubuf.shape[1]
    rows = ubuf[pl.ds(start, count * KZ), :].astype(jnp.bfloat16)
    timed = dot32(rows, t_table)
    pieces = []
    for y in range(count):
        mine = timed[y * KZ : (y + 1) * KZ]
        pieces.append(
            jnp.concatenate([mine[:, :lanes], mine[:, lanes:]], axis=0).astype(jnp.bfloat16)
        )
    return pieces


def write_blocks(spec, out_ref, own, stats):
    devices, padded, lanes = out_ref.shape
    spare = padded - own
    if spare > 1:
        zeros = jnp.zeros((spare - 1, lanes), jnp.float32)
        tail = jnp.concatenate([stats, zeros], axis=0)
    else:
        tail = stats
    for d in range(devices):
        out_ref[d, 0:own, :] = spec[d * own : (d + 1) * own, :]
        out_ref[d, own:padded, :] = tail


def read_blocks(in_ref, spec, own, scale):
    for d in range(in_ref.shape[0]):
        spec[d * own : (d + 1) * own, :] = in_ref[d, 0:own, :] * scale


def spectrum_kernel(count, own, f_ref, zt_ref, tt_ref, yt_ref, out_ref, zbuf, spec):
    step = pl.program_id(0)
    lanes = zbuf.shape[1]
    chunk = z_forward(lambda y: f_ref[y], count, zt_ref[...], tt_ref[...])
    zbuf[pl.ds(pl.multiple_of(step * (count * KZ), 8), count * KZ), :] = chunk

    @pl.when(step == pl.num_programs(0) - 1)
    def _():
        y_forward(zbuf, spec, yt_ref[...], zbuf.shape[0] // KZ, lanes)
        write_blocks(spec, out_ref, own, jnp.zeros((1, lanes), jnp.float32))


def activation_kernel(
    count,
    own,
    scale,
    channels,
    in_ref,
    f_ref,
    cot_ref,
    skip_ref,
    bias_ref,
    yb_ref,
    tb_ref,
    zb_ref,
    zt_ref,
    tt_ref,
    yt_ref,
    out_ref,
    grad_ref,
    send_ref,
    ubuf,
    zbuf,
    spec,
    outer,
    total_row,
):
    step = pl.program_id(0)
    lanes = ubuf.shape[1]
    rows_y = ubuf.shape[0] // KZ

    @pl.when(step == 0)
    def _():
        read_blocks(in_ref, spec, own, scale)
        y_backward(spec, ubuf, yb_ref[...], rows_y, lanes)
        outer[...] = jnp.zeros_like(outer)
        total_row[...] = jnp.zeros_like(total_row)

    start = pl.multiple_of(step * (count * KZ), 8)
    pieces = z_backward(ubuf, start, count, tb_ref[...])
    bias_row = bias_ref[...]
    for y in range(count):
        field = f_ref[y]
        pre = dot32(zb_ref[...], pieces[y]) + dot32(field, skip_ref[...]) + bias_row
        cdf = 0.5 * (1.0 + lax.erf(pre * (1.0 / math.sqrt(2.0))))
        pdf = jnp.exp(-0.5 * pre * pre) * (1.0 / math.sqrt(2.0 * math.pi))
        out_ref[y] = (pre * cdf).astype(jnp.bfloat16)
        slope = cdf + pre * pdf
        grad = (cot_ref[y].astype(jnp.float32) * slope).astype(jnp.bfloat16)
        grad_ref[y] = grad
        total_row[...] += jnp.sum(
            grad.astype(jnp.float32).reshape(-1, 8, lanes), axis=0
        )
    flat_f = f_ref[...].reshape(-1, lanes)
    flat_g = grad_ref[...].reshape(-1, lanes)
    outer[...] += lax.dot_general(
        flat_f, flat_g, (((0,), (0,)), ((), ())), preferred_element_type=jnp.float32
    )
    chunk = z_forward(lambda y: grad_ref[y], count, zt_ref[...], tt_ref[...])
    zbuf[pl.ds(start, count * KZ), :] = chunk

    @pl.when(step == pl.num_programs(0) - 1)
    def _():
        y_forward(zbuf, spec, yt_ref[...], rows_y, lanes)
        row = lax.broadcasted_iota(jnp.int32, (lanes, lanes), 0)
        lane = lax.broadcasted_iota(jnp.int32, (lanes, lanes), 1)
        same_t = row // channels == lane // channels
        same_c = (row % channels == lane % channels).astype(jnp.float32)
        diagonal = jnp.where(same_t, outer[...], 0.0)
        per_c = jnp.dot(diagonal, same_c, precision=FULL_PRECISION)
        keep = (row % channels) == (lane // channels)
        skip_row = jnp.sum(jnp.where(keep, per_c, 0.0), axis=0, keepdims=True)
        folded = jnp.dot(total_row[...], same_c, precision=FULL_PRECISION)
        group = lax.broadcasted_iota(jnp.int32, (1, lanes), 1) // channels
        bias_sum = jnp.sum(folded, axis=0, keepdims=True)
        bias_sum = jnp.where(group == channels, bias_sum, 0.0)
        write_blocks(spec, send_ref, own, skip_row + bias_sum)


def field_grad_kernel(
    count, own, scale, in_ref, grad_ref, skip_ref, yb_ref, tb_ref, zb_ref, out_ref, ubuf, spec
):
    step = pl.program_id(0)
    lanes = ubuf.shape[1]

    @pl.when(step == 0)
    def _():
        read_blocks(in_ref, spec, own, scale)
        y_backward(spec, ubuf, yb_ref[...], ubuf.shape[0] // KZ, lanes)

    start = pl.multiple_of(step * (count * KZ), 8)
    pieces = z_backward(ubuf, start, count, tb_ref[...])
    for y in range(count):
        value = dot32(zb_ref[...], pieces[y]) + dot32(grad_ref[y], skip_ref[...])
        out_ref[y] = value.astype(jnp.bfloat16)


def x_forward(in_ref, tile, x_table):
    devices, _, lanes = in_ref.shape
    block = in_ref[:, tile * PAD_ROWS : (tile + 1) * PAD_ROWS, :]
    block = block.reshape(devices * PAD_ROWS, lanes)
    high, low = split_pair(block)
    both = dot32(x_table, jnp.concatenate([high, low, high], axis=0))
    rows = PAD_ROWS * KX
    return both[:rows] + half_sign((rows, lanes), 1.0, -1.0) * roll_half(both[rows:])


def x_backward(columns, out_ref, tile, x_table):
    devices, _, lanes = out_ref.shape
    missing = PAD_ROWS * KX - columns.shape[0]
    if missing:
        columns = jnp.concatenate([columns, jnp.zeros((missing, lanes), jnp.float32)], axis=0)
    turned = half_sign(columns.shape, -1.0, 1.0) * roll_half(columns)
    high, low = split_pair(jnp.concatenate([columns, turned], axis=0))
    size = devices * PAD_ROWS
    from_high = dot32(x_table, high)
    rows = from_high[:size] + from_high[size:] + dot32(x_table[:size], low)
    out_ref[:, tile * PAD_ROWS : (tile + 1) * PAD_ROWS, :] = rows.reshape(
        devices, PAD_ROWS, lanes
    )


def mixed_rows(spectrum, w_ref, first, pairs, pick_ref, fold_ref):
    wide = w_ref.shape[3]
    high, low = split_pair(spectrum)
    doubled = jnp.concatenate([high, low], axis=1)
    total = None
    for k in range(KT):
        terms = dot32(doubled, pick_ref[k])
        weight = w_ref[first : first + pairs, k].astype(jnp.float32).reshape(pairs * KX, wide)
        product = jnp.concatenate([terms[:, :wide] * weight, terms[:, wide:] * weight], axis=1)
        part = dot32(product.astype(jnp.bfloat16), fold_ref[k])
        total = part if total is None else total + part
    return total


def mix_kernel(with_stats, in_ref, w_ref, xf_ref, xb_ref, pick_ref, fold_ref, *outs):
    spectrum_ref, send_ref = outs[:2]
    own = w_ref.shape[0]
    rows = PAD_ROWS * KX
    for tile in range(pl.cdiv(own, PAD_ROWS)):
        first = tile * PAD_ROWS
        pairs = min(PAD_ROWS, own - first)
        spectrum = x_forward(in_ref, tile, xf_ref[...])
        spectrum_ref[tile * rows : (tile + 1) * rows, :] = spectrum
        mixed = mixed_rows(spectrum[: pairs * KX], w_ref, first, pairs, pick_ref, fold_ref)
        x_backward(mixed, send_ref, tile, xb_ref[...])
    for tile in range(pl.cdiv(own, PAD_ROWS), in_ref.shape[1] // PAD_ROWS):
        lanes = send_ref.shape[2]
        send_ref[:, tile * PAD_ROWS : (tile + 1) * PAD_ROWS, :] = jnp.zeros(
            (send_ref.shape[0], PAD_ROWS, lanes), jnp.float32
        )
    if with_stats:
        outs[2][...] = jnp.sum(in_ref[:, own, :], axis=0, keepdims=True)


def weight_gradient_kernel(scale, s_ref, t_ref, ps_ref, pt_ref, out_ref):
    pairs, _, _, wide = out_ref.shape
    for_s = jnp.concatenate(split_pair(s_ref[...]), axis=1)
    for_t = jnp.concatenate(split_pair(t_ref[...] * scale), axis=1)
    for k in range(KT):
        left = dot32(for_s, ps_ref[k])
        right = dot32(for_t, pt_ref[k])
        value = left[:, :wide] * right[:, :wide] + left[:, wide:] * right[:, wide:]
        out_ref[:, k] = value.reshape(pairs, KX, wide)


def whole(array):
    zeros = (0,) * array.ndim
    return pl.BlockSpec(array.shape, lambda *_: zeros)


def params(**extra):
    return pltpu.CompilerParams(vmem_limit_bytes=48 * 1024 * 1024, **extra)


def fast_device(field, cotangent, spectral_weight, skip_weight, bias):
    _, rows_y, rows_z, lanes = field.shape
    channels = skip_weight.shape[0]
    steps_t = lanes // channels
    devices = lax.axis_size("space")
    total = devices * rows_y * rows_z * steps_t
    scale = 1.0 / total
    own = KY * KZ // devices
    padded = (own // PAD_ROWS + 1) * PAD_ROWS
    wide = spectral_weight.shape[2]
    t = make_tables(rows_y, rows_z, steps_t, channels, devices)
    count = 16
    while rows_y % count:
        count //= 2
    steps = rows_y // count
    field = field.reshape(rows_y, rows_z, lanes)
    cotangent = cotangent.reshape(rows_y, rows_z, lanes)
    weights = spectral_weight.reshape(own, KT, KX, wide)
    skip_f32 = skip_weight.astype(jnp.float32)
    skip_table = block_diagonal(skip_f32, steps_t).astype(jnp.bfloat16)
    skip_back = block_diagonal(skip_f32.T, steps_t).astype(jnp.bfloat16)
    bias_row = jnp.tile(bias.astype(jnp.float32), steps_t).reshape(1, lanes)
    plane_spec = pl.BlockSpec((count, rows_z, lanes), lambda i: (i, 0, 0))
    plane_shape = jax.ShapeDtypeStruct((rows_y, rows_z, lanes), jnp.bfloat16)
    block_shape = jax.ShapeDtypeStruct((devices, padded, lanes), jnp.float32)
    block_spec = pl.BlockSpec((devices, padded, lanes), lambda *_: (0, 0, 0))
    mode_rows = pl.cdiv(own, PAD_ROWS) * PAD_ROWS * KX
    spectrum_shape = jax.ShapeDtypeStruct((mode_rows, lanes), jnp.float32)
    plane_buf = pltpu.VMEM((rows_y * KZ, lanes), jnp.float32)
    spec_buf = pltpu.VMEM((KY * KZ, lanes), jnp.float32)

    def exchange(blocks):
        return lax.all_to_all(blocks, "space", split_axis=0, concat_axis=0, tiled=True)

    operands = (field, t["z_fwd"], t["t_fwd"], t["y_fwd"])
    sent = pl.pallas_call(
        functools.partial(spectrum_kernel, count, own),
        grid=(steps,),
        in_specs=[plane_spec] + [whole(x) for x in operands[1:]],
        out_specs=block_spec,
        out_shape=block_shape,
        scratch_shapes=[plane_buf, spec_buf],
        compiler_params=params(),
        name="field_spectrum",
    )(*operands)
    own_field, sent = pl.pallas_call(
        functools.partial(mix_kernel, False),
        out_shape=[spectrum_shape, block_shape],
        compiler_params=params(),
        name="mix_forward",
    )(exchange(sent), weights, t["x_fwd"], t["x_back"], t["pick_s"], t["fold_s"])
    operands = (
        exchange(sent),
        field,
        cotangent,
        skip_table,
        bias_row,
        t["y_back"],
        t["t_back"],
        t["z_back"],
        t["z_fwd"],
        t["t_fwd"],
        t["y_fwd"],
    )
    output, grad_pre, sent = pl.pallas_call(
        functools.partial(activation_kernel, count, own, scale, channels),
        grid=(steps,),
        in_specs=[whole(operands[0]), plane_spec, plane_spec] + [whole(x) for x in operands[3:]],
        out_specs=[plane_spec, plane_spec, block_spec],
        out_shape=[plane_shape, plane_shape, block_shape],
        scratch_shapes=[
            plane_buf,
            plane_buf,
            spec_buf,
            pltpu.VMEM((lanes, lanes), jnp.float32),
            pltpu.VMEM((8, lanes), jnp.float32),
        ],
        compiler_params=params(),
        name="activation",
    )(*operands)
    own_grad, sent, stats = pl.pallas_call(
        functools.partial(mix_kernel, True),
        out_shape=[spectrum_shape, block_shape, jax.ShapeDtypeStruct((1, lanes), jnp.float32)],
        compiler_params=params(),
        name="mix_adjoint",
    )(exchange(sent), weights, t["x_fwd"], t["x_back"], t["pick_t"], t["fold_t"])
    arrived = exchange(sent)
    pairs = 4 if own % 4 == 0 else 1
    mode_spec = pl.BlockSpec((pairs * KX, lanes), lambda i: (i, 0))
    spectral_grad = pl.pallas_call(
        functools.partial(weight_gradient_kernel, scale),
        grid=(own // pairs,),
        in_specs=[mode_spec, mode_spec, whole(t["pick_s"]), whole(t["pick_t"])],
        out_specs=pl.BlockSpec((pairs, KT, KX, wide), lambda i: (i, 0, 0, 0)),
        out_shape=jax.ShapeDtypeStruct((own, KT, KX, wide), jnp.float32),
        compiler_params=params(),
        cost_estimate=pl.CostEstimate(
            flops=4 * own * KX * KT * 65536, bytes_accessed=8 * own * KX * KT * wide, transcendentals=0
        ),
        name="weight_gradient",
    )(own_field, own_grad, t["pick_s"], t["pick_t"])
    operands = (arrived, grad_pre, skip_back, t["y_back"], t["t_back"], t["z_back"])
    field_grad = pl.pallas_call(
        functools.partial(field_grad_kernel, count, own, scale),
        grid=(steps,),
        in_specs=[whole(operands[0]), plane_spec] + [whole(x) for x in operands[2:]],
        out_specs=plane_spec,
        out_shape=plane_shape,
        scratch_shapes=[plane_buf, spec_buf],
        compiler_params=params(),
        name="field_grad",
    )(*operands)
    root = 1.0 / math.sqrt(total)
    square = channels * channels
    skip_grad = stats[0, :square].reshape(channels, channels) * root
    bias_grad = stats[0, square : square + channels] * root
    return (
        output[None],
        field_grad[None],
        spectral_grad.reshape(own * KT, KX, wide),
        skip_grad,
        bias_grad,
    )


def on_any_device(field, cotangent, spectral_weight, skip_weight, bias):
    devices = lax.axis_size("space")
    channels = skip_weight.shape[0]
    fits = (
        field.shape[0] == 1
        and (KY * KZ) % devices == 0
        and devices <= 32
        and field.shape[3] == 2 * KT * channels
        and channels * channels + channels <= field.shape[3]
        and spectral_weight.shape[2] == field.shape[3]
    )
    body = fast_device if fits else on_device
    return body(field, cotangent, spectral_weight, skip_weight, bias)


def solution(mesh):
    in_specs = (
        P(("groups", "space"), None, None, None),
        P(("groups", "space"), None, None, None),
        P("space", None, None),
        P(),
        P(),
    )
    out_specs = (
        P(("groups", "space"), None, None, None),
        P(("groups", "space"), None, None, None),
        P(("groups", "space"), None, None),
        P("groups", None),
        P("groups"),
    )
    return jax.shard_map(
        on_any_device, mesh=mesh, in_specs=in_specs, out_specs=out_specs, check_vma=False
    )
```

profile of v0, /device:TPU:0, one launch (start us, length us, event | category | flops | bytes accessed | tf_op | source)
XLA Modules:
  0.0 103.5 jit_solution(50992057423651156)
XLA Ops:
  0.6 0.0 copy-start
  0.6 1.7 %copy-done = bf16[1,96,96,128]{3,2,1,0:T(8,128)(2,1)S(1)} copy-done((bf16[1,96,96,128]{3,2,1,0:T(8,128)(2,1)S(1)}, bf16[1,96,96,128]{3,2,1,0:T(8,128)(2,1)}, u32[]{:S(2)}) %copy-start) | copy-done | bytes 2359320
  2.3 0.8 copy-done.15
  3.1 0.7 copy-done.18
  3.9 2.7 %field_spectrum.1 = f32[16,40,128]{2,1,0:T(8,128)S(1)} custom-call(bf16[96,96,128]{2,1,0:T(8,128)(2,1)S(1)} %bitcast.14, bf16[48,96]{1,0:T(8,128)(2,1)S(1)} %copy-done.18, bf16[256,128]{1,0:T(8,128)(2,1)S(1)} %copy-done.15, bf16[48,96]{1,0:T(8,128)(2,1)S(1)} %copy-done.18), custom_call_target="tpu_custom_call" | custom-call | tf_op jit(solution)/shard_map/field_spectrum/pallas_call | solution.py:616
  6.6 18.3 %all_to_all.20.in_ref = f32[16,40,128]{2,1,0:T(8,128)S(1)} all-to-all(f32[16,40,128]{2,1,0:T(8,128)S(1)} %field_spectrum.1), channel_id=1, replica_groups=mesh['groups'=2,'space'=16] {'space'}, dimensions={0} | all-to-all | bytes 655360 | tf_op jit(solution)/shard_map/all_to_all | solution.py:613
  24.8 0.0 copy-done.2
  24.8 0.0 copy-done.6
  24.8 0.0 copy-done.7
  24.8 0.0 copy-done.11
  24.8 0.0 copy-start.13
  24.9 1.0 copy-done.13
  25.9 0.0 copy-start.16
  25.9 0.0 copy-start.17
  25.9 0.0 copy-start.19
  25.9 0.0 copy-start.20
  26.0 7.2 %mix_forward.1 = (f32[960,128]{1,0:T(8,128)S(1)}, f32[16,40,128]{2,1,0:T(8,128)}) custom-call(f32[16,40,128]{2,1,0:T(8,128)S(1)} %all_to_all.20.in_ref, bf16[36,8,24,128]{3,2,1,0:T(8,128)(2,1)S(1)} %bitcast.16, bf16[384,384]{1,0:T(8,128)(2,1)S(1)} %copy-done.6, bf16[256,384]{1,0:T(8,128)(2,1)S(1)} %copy-done.11, bf16[8,256,256]{2,1,0:T(8,128)(2,1)S(1)} %copy-done.7, ...), custom_call_target="tpu_custom_call" | custom-call | tf_op jit(solution)/shard_map/mix_forward/pallas_call | solution.py:626
  33.1 0.8 copy-done.21
  33.9 3.5 %all-to-all-start.1 = ((f32[16,40,128]{2,1,0:T(8,128)}), f32[16,40,128]{2,1,0:T(8,128)S(1)}, u32[]{:S(2)}, u32[]{:S(2)}) async-start(f32[16,40,128]{2,1,0:T(8,128)} %get-tuple-element.13), calls=%async_computation.1 | async-start | bytes 655360 | tf_op jit(solution)/shard_map/all_to_all | solution.py:613
  37.4 0.0 copy-done.26
  37.5 0.1 copy.23
  37.5 1.2 %multiply_convert_fusion = (bf16[16,8,16,8]{3,2,1,0:T(8,128)(2,1)}, bf16[16,8,16,8]{3,2,1,0:T(8,128)(2,1)}) fusion(f32[8,8]{1,0:T(8,128)S(1)} %copy.23, f32[16,16]{1,0:T(8,128)S(1)} %fusion, f32[8,8]{1,0:T(8,128)S(1)} %get-tuple-element.24), kind=kLoop, calls=%fused_computation | loop fusion | flops 65536 | bytes 67072 | tf_op jit(solution)/shard_map/convert_element_type | solution.py:601
  38.8 1.5 %convert_element_type.29.skip_ref = bf16[128,128]{1,0:T(8,128)(2,1)S(1)} reshape(bf16[16,8,16,8]{3,2,1,0:T(8,128)(2,1)} %get-tuple-element.22) | data formatting | bytes 65536 | tf_op jit(solution)/shard_map/convert_element_type | solution.py:600
  40.2 0.0 copy-done.27
  40.3 0.1 reshape_tile.3.bias_ref
  40.4 8.1 %all-to-all-done.1.in_ref = f32[16,40,128]{2,1,0:T(8,128)S(1)} async-done(((f32[16,40,128]{2,1,0:T(8,128)}), f32[16,40,128]{2,1,0:T(8,128)S(1)}, u32[]{:S(2)}, u32[]{:S(2)}) %all-to-all-start.1) | async-done | bytes 327712 | tf_op jit(solution)/shard_map/all_to_all | solution.py:613
  48.5 0.0 copy-start.3
  48.6 0.0 copy-start.9
  48.6 0.0 copy-start.12
  48.6 10.3 %activation.1 = (bf16[96,96,128]{2,1,0:T(8,128)(2,1)}, bf16[96,96,128]{2,1,0:T(8,128)(2,1)S(1)}, f32[16,40,128]{2,1,0:T(8,128)S(1)}) custom-call(f32[16,40,128]{2,1,0:T(8,128)S(1)} %all-to-all-done.1.in_ref, bf16[96,96,128]{2,1,0:T(8,128)(2,1)S(1)} %bitcast.15, bf16[96,96,128]{2,1,0:T(8,128)(2,1)} %bitcast.19, ...), custom_call_target="tpu_custom_call" | custom-call | tf_op jit(solution)/shard_map/activation/pallas_call | solution.py:645
  58.9 1.4 %copy-done.4 = bf16[96,96,128]{2,1,0:T(8,128)(2,1)} copy-done((bf16[96,96,128]{2,1,0:T(8,128)(2,1)}, bf16[96,96,128]{2,1,0:T(8,128)(2,1)S(1)}, u32[]{:S(2)}) %copy-start.4) | copy-done | bytes 2359320
  60.3 14.1 %all_to_all.21.in_ref = f32[16,40,128]{2,1,0:T(8,128)S(1)} all-to-all(f32[16,40,128]{2,1,0:T(8,128)S(1)} %get-tuple-element.15), channel_id=1, replica_groups=mesh['groups'=2,'space'=16] {'space'}, dimensions={0} | all-to-all | bytes 655360 | tf_op jit(solution)/shard_map/all_to_all | solution.py:613
  74.4 0.0 copy-done.3
  74.4 0.0 copy-done.12
  74.4 0.0 copy-start.25
  74.4 7.2 %mix_adjoint.1 = (f32[960,128]{1,0:T(8,128)S(1)}, f32[16,40,128]{2,1,0:T(8,128)}, f32[1,128]{1,0:T(1,128)S(1)}) custom-call(f32[16,40,128]{2,1,0:T(8,128)S(1)} %all_to_all.21.in_ref, bf16[36,8,24,128]{3,2,1,0:T(8,128)(2,1)S(1)} %bitcast.17, bf16[384,384]{1,0:T(8,128)(2,1)S(1)} %copy-done.6, bf16[256,384]{1,0:T(8,128)(2,1)S(1)} %copy-done.11, ...), custom_call_target="tpu_custom_call" | custom-call | tf_op jit(solution)/shard_map/mix_adjoint/pallas_call | solution.py:661
  81.6 0.8 copy-done.23
  82.4 3.5 %all-to-all-start.3 = ((f32[16,40,128]{2,1,0:T(8,128)}), f32[16,40,128]{2,1,0:T(8,128)S(1)}, u32[]{:S(2)}, u32[]{:S(2)}) async-start(f32[16,40,128]{2,1,0:T(8,128)} %get-tuple-element.16), calls=%async_computation.3 | async-start | bytes 655360 | tf_op jit(solution)/shard_map/all_to_all | solution.py:613
  85.9 0.5 convert_element_type.32.skip_ref
  86.5 0.7 mul.52
  87.2 1.2 %copy-done.8 = bf16[8,256,256]{2,1,0:T(8,128)(2,1)S(1)} copy-done((bf16[8,256,256]{2,1,0:T(8,128)(2,1)S(1)}, bf16[8,256,256]{2,1,0:T(8,128)(2,1)}, u32[]{:S(2)}) %copy-start.8) | copy-done | bytes 1048600
  88.4 1.2 %copy-done.10 = bf16[8,256,256]{2,1,0:T(8,128)(2,1)S(1)} copy-done((bf16[8,256,256]{2,1,0:T(8,128)(2,1)S(1)}, bf16[8,256,256]{2,1,0:T(8,128)(2,1)}, u32[]{:S(2)}) %copy-start.10) | copy-done | bytes 1048600
  89.6 1.0 copy-done.22
  90.6 1.0 copy-done.24
  91.7 6.1 %weight_gradient.1 = f32[36,8,24,128]{3,2,1,0:T(8,128)} custom-call(f32[960,128]{1,0:T(8,128)S(1)} %copy-done.22, f32[960,128]{1,0:T(8,128)S(1)} %copy-done.24, bf16[8,256,256]{2,1,0:T(8,128)(2,1)S(1)} %copy-done.8, bf16[8,256,256]{2,1,0:T(8,128)(2,1)S(1)} %copy-done.10), custom_call_target="tpu_custom_call" | custom-call | flops 1811939328 | bytes 7077888 | tf_op jit(solution)/shard_map/weight_gradient/pallas_call | solution.py:670
  97.8 0.6 multiply_bitcast_fusion
  98.3 0.0 all-to-all-done.3.in_ref
  98.4 5.1 %field_grad.1 = bf16[96,96,128]{2,1,0:T(8,128)(2,1)} custom-call(f32[16,40,128]{2,1,0:T(8,128)S(1)} %all-to-all-done.3.in_ref, bf16[96,96,128]{2,1,0:T(8,128)(2,1)S(1)} %copy-done.5, bf16[128,128]{1,0:T(8,128)(2,1)S(1)} %convert_element_type.32.skip_ref, bf16[96,144]{1,0:T(8,128)(2,1)S(1)} %copy-done.17, bf16[128,256]{1,0:T(8,128)(2,1)S(1)} %copy-done.14, ...), custom_call_target="tpu_custom_call" | custom-call | tf_op jit(solution)/shard_map/field_grad/pallas_call | solution.py:683
  (31 shorter events, 0.1 us)
Async XLA Ops:
  0.6 1.7 %copy-start = (bf16[1,96,96,128]{3,2,1,0:T(8,128)(2,1)S(1)}, bf16[1,96,96,128]{3,2,1,0:T(8,128)(2,1)}, u32[]{:S(2)}) copy-start(bf16[1,96,96,128]{3,2,1,0:T(8,128)(2,1)} %param.17) | copy-start | bytes 7077892
  2.3 0.8 copy-start.15
  3.1 0.7 copy-start.18
  3.8 21.0 %copy-start.2 = (bf16[288,24,128]{2,1,0:T(8,128)(2,1)S(1)}, bf16[288,24,128]{2,1,0:T(8,128)(2,1)}, u32[]{:S(2)}) copy-start(bf16[288,24,128]{2,1,0:T(8,128)(2,1)} %param.19) | copy-start | bytes 5308420
  3.8 21.0 %copy-start.6 = (bf16[384,384]{1,0:T(8,128)(2,1)S(1)}, bf16[384,384]{1,0:T(8,128)(2,1)}, u32[]{:S(2)}) copy-start(bf16[384,384]{1,0:T(8,128)(2,1)} %constant.30.clone.xf_ref) | copy-start | bytes 884740
  3.9 21.0 %copy-start.7 = (bf16[8,256,256]{2,1,0:T(8,128)(2,1)S(1)}, bf16[8,256,256]{2,1,0:T(8,128)(2,1)}, u32[]{:S(2)}) copy-start(bf16[8,256,256]{2,1,0:T(8,128)(2,1)} %constant.32.clone.pick_ref.ps_ref) | copy-start | bytes 3145732
  3.9 21.0 %copy-start.11 = (bf16[256,384]{1,0:T(8,128)(2,1)S(1)}, bf16[256,384]{1,0:T(8,128)(2,1)}, u32[]{:S(2)}) copy-start(bf16[256,384]{1,0:T(8,128)(2,1)} %constant.31.clone.xb_ref) | copy-start | bytes 589828
  24.8 1.0 %copy-start.13 = (bf16[8,256,128]{2,1,0:T(8,128)(2,1)S(1)}, bf16[8,256,128]{2,1,0:T(8,128)(2,1)}, u32[]{:S(2)}) copy-start(bf16[8,256,128]{2,1,0:T(8,128)(2,1)} %constant.34.clone.fold_ref) | copy-start | bytes 1572868
  25.9 11.6 %copy-start.26 = (bf16[8,8]{1,0:T(8,128)(2,1)S(1)}, bf16[8,8]{1,0:T(8,128)(2,1)}, u32[]{:S(2)}) copy-start(bf16[8,8]{1,0:T(8,128)(2,1)} %param.20) | copy-start | bytes 388
  25.9 14.4 %copy-start.27 = (bf16[8]{0:T(256)(128)(2,1)S(1)}, bf16[8]{0:T(256)(128)(2,1)}, u32[]{:S(2)}) copy-start(bf16[8]{0:T(256)(128)(2,1)} %param.21) | copy-start | bytes 52
  25.9 22.6 %copy-start.1 = (bf16[1,96,96,128]{3,2,1,0:T(8,128)(2,1)S(1)}, bf16[1,96,96,128]{3,2,1,0:T(8,128)(2,1)}, u32[]{:S(2)}) copy-start(bf16[1,96,96,128]{3,2,1,0:T(8,128)(2,1)} %param.17) | copy-start | bytes 7077892
  25.9 22.6 %copy-start.14 = (bf16[128,256]{1,0:T(8,128)(2,1)S(1)}, bf16[128,256]{1,0:T(8,128)(2,1)}, u32[]{:S(2)}) copy-start(bf16[128,256]{1,0:T(8,128)(2,1)} %constant.28.clone.tb_ref) | copy-start | bytes 196612
  25.9 22.6 %copy-start.16 = (bf16[256,128]{1,0:T(8,128)(2,1)S(1)}, bf16[256,128]{1,0:T(8,128)(2,1)}, u32[]{:S(2)}) copy-start(bf16[256,128]{1,0:T(8,128)(2,1)} %constant.26.clone.tt_ref) | copy-start | bytes 196612
  25.9 22.6 %copy-start.17 = (bf16[96,144]{1,0:T(8,128)(2,1)S(1)}, bf16[96,144]{1,0:T(8,128)(2,1)}, u32[]{:S(2)}) copy-start(bf16[96,144]{1,0:T(8,128)(2,1)} %constant.27.clone.yb_ref) | copy-start | bytes 82948
  25.9 22.6 %copy-start.19 = (bf16[48,96]{1,0:T(8,128)(2,1)S(1)}, bf16[48,96]{1,0:T(8,128)(2,1)}, u32[]{:S(2)}) copy-start(bf16[48,96]{1,0:T(8,128)(2,1)} %constant.11.clone.zt_ref.yt_ref) | copy-start | bytes 27652
  25.9 22.6 %copy-start.20 = (bf16[96,48]{1,0:T(8,128)(2,1)S(1)}, bf16[96,48]{1,0:T(8,128)(2,1)}, u32[]{:S(2)}) copy-start(bf16[96,48]{1,0:T(8,128)(2,1)} %constant.29.clone.zb_ref) | copy-start | bytes 27652
  33.1 0.8 copy-start.21
  33.9 14.6 %all-to-all-start.1 = ((f32[16,40,128]{2,1,0:T(8,128)}), f32[16,40,128]{2,1,0:T(8,128)S(1)}, u32[]{:S(2)}, u32[]{:S(2)}) async-start(f32[16,40,128]{2,1,0:T(8,128)} %get-tuple-element.13), calls=%async_computation.1 | async-start | bytes 655360 | tf_op jit(solution)/shard_map/all_to_all | solution.py:613
  48.5 25.8 %copy-start.3 = (bf16[288,24,128]{2,1,0:T(8,128)(2,1)S(1)}, bf16[288,24,128]{2,1,0:T(8,128)(2,1)}, u32[]{:S(2)}) copy-start(bf16[288,24,128]{2,1,0:T(8,128)(2,1)} %param.19) | copy-start | bytes 5308420
  48.6 25.8 %copy-start.9 = (bf16[8,256,256]{2,1,0:T(8,128)(2,1)S(1)}, bf16[8,256,256]{2,1,0:T(8,128)(2,1)}, u32[]{:S(2)}) copy-start(bf16[8,256,256]{2,1,0:T(8,128)(2,1)} %constant.33.clone.pick_ref.pt_ref) | copy-start | bytes 3145732
  48.6 25.8 %copy-start.12 = (bf16[8,256,128]{2,1,0:T(8,128)(2,1)S(1)}, bf16[8,256,128]{2,1,0:T(8,128)(2,1)}, u32[]{:S(2)}) copy-start(bf16[8,256,128]{2,1,0:T(8,128)(2,1)} %constant.35.clone.fold_ref) | copy-start | bytes 1572868
  58.9 1.4 %copy-start.4 = (bf16[96,96,128]{2,1,0:T(8,128)(2,1)}, bf16[96,96,128]{2,1,0:T(8,128)(2,1)S(1)}, u32[]{:S(2)}) copy-start(bf16[96,96,128]{2,1,0:T(8,128)(2,1)S(1)} %get-tuple-element.17.grad_ref) | copy-start | bytes 7077892
  74.4 11.5 %copy-start.25 = (bf16[16,8,16,8]{3,2,1,0:T(8,128)(2,1)S(1)}, bf16[16,8,16,8]{3,2,1,0:T(8,128)(2,1)}, u32[]{:S(2)}) copy-start(bf16[16,8,16,8]{3,2,1,0:T(8,128)(2,1)} %get-tuple-element.21) | copy-start | bytes 98308
  81.6 0.8 copy-start.23
  82.4 16.0 %all-to-all-start.3 = ((f32[16,40,128]{2,1,0:T(8,128)}), f32[16,40,128]{2,1,0:T(8,128)S(1)}, u32[]{:S(2)}, u32[]{:S(2)}) async-start(f32[16,40,128]{2,1,0:T(8,128)} %get-tuple-element.16), calls=%async_computation.3 | async-start | bytes 655360 | tf_op jit(solution)/shard_map/all_to_all | solution.py:613
  87.2 1.2 %copy-start.8 = (bf16[8,256,256]{2,1,0:T(8,128)(2,1)S(1)}, bf16[8,256,256]{2,1,0:T(8,128)(2,1)}, u32[]{:S(2)}) copy-start(bf16[8,256,256]{2,1,0:T(8,128)(2,1)} %constant.32.clone.pick_ref.ps_ref) | copy-start | bytes 3145732
  88.4 1.2 %copy-start.10 = (bf16[8,256,256]{2,1,0:T(8,128)(2,1)S(1)}, bf16[8,256,256]{2,1,0:T(8,128)(2,1)}, u32[]{:S(2)}) copy-start(bf16[8,256,256]{2,1,0:T(8,128)(2,1)} %constant.33.clone.pick_ref.pt_ref) | copy-start | bytes 3145732
  89.6 1.0 copy-start.22
  90.6 1.0 copy-start.24
  91.7 6.7 %copy-start.5 = (bf16[96,96,128]{2,1,0:T(8,128)(2,1)S(1)}, bf16[96,96,128]{2,1,0:T(8,128)(2,1)}, u32[]{:S(2)}) copy-start(bf16[96,96,128]{2,1,0:T(8,128)(2,1)} %copy-done.4) | copy-start | bytes 7077892
where the time goes:
time: 104 us; the launch traced here: 103 us
  Pallas kernels  38.5 us (37%)
  blocking collectives  32.4 us (31%)
  local copies, waits for them, and re-layouts  14.7 us (14%)
  waiting for transfers between devices  8.15 us (8%)
  starting transfers between devices  7.08 us (7%)
  other arithmetic  1.82 us (2%)
    all_to_all x2, blocking collectives, exchange(): lax.all_to_all(blocks, 'space', split_axis=0, concat_axis=0, tiled=True)  32.4 us
    unnamed x56, local copies, waits for them, and re-layouts  11.8 us
    pallas_call x1, Pallas kernels, fast_device(): pl.pallas_call(functools.partial(activation_kernel, count, own, scale, ch...  10.3 us
    all_to_all x2, waiting for transfers between devices, exchange(): lax.all_to_all(blocks, 'space', split_axis=0, concat_axis=0, tiled=True)  8.15 us
    pallas_call x1, Pallas kernels, fast_device(): pl.pallas_call(functools.partial(mix_kernel, False), out_shape=[spectrum_...  7.16 us
    pallas_call x1, Pallas kernels, fast_device(): pl.pallas_call(functools.partial(mix_kernel, True), out_shape=[spectrum_s...  7.15 us
    all_to_all x2, starting transfers between devices, exchange(): lax.all_to_all(blocks, 'space', split_axis=0, concat_axis=0, tiled=True)  7.08 us
    pallas_call x1, Pallas kernels, fast_device(): pl.pallas_call(functools.partial(weight_gradient_kernel, scale), grid=(ow...  6.1 us
  transfers between devices with their start and end apart: 2, of which 1 were waited for; matrix products, arithmetic and copies ran while one was open for 5% of the time, Pallas kernels for 6%

commit v1 on v0

--- a/solution.py
+++ b/solution.py
@@ -392,8 +392,153 @@
         spec[d * own : (d + 1) * own, :] = in_ref[d, 0:own, :] * scale
 
 
-def spectrum_kernel(count, own, f_ref, zt_ref, tt_ref, yt_ref, out_ref, zbuf, spec):
+def greet_all():
+    devices = lax.axis_size("space")
+    me = lax.axis_index("space")
+    barrier = pltpu.get_barrier_semaphore()
+
+    def signal(offset, carry):
+        peer = lax.rem(me + offset, devices)
+        pl.semaphore_signal(
+            barrier, inc=1, device_id={"space": peer}, device_id_type=pl.DeviceIdType.MESH
+        )
+        return carry
+
+    lax.fori_loop(1, devices, signal, 0)
+
+
+def await_all():
+    pl.semaphore_wait(pltpu.get_barrier_semaphore(), lax.axis_size("space") - 1)
+
+
+def peer_copy(offset, part, rows, send, recv, send_sems, recv_sems):
+    devices = lax.axis_size("space")
+    me = lax.axis_index("space")
+    peer = lax.rem(me + offset, devices)
+    low, high = rows
+    return pltpu.make_async_remote_copy(
+        src_ref=send.at[peer, low:high],
+        dst_ref=recv.at[me, low:high],
+        send_sem=send_sems.at[part, offset],
+        recv_sem=recv_sems.at[part, offset],
+        device_id={"space": peer},
+        device_id_type=pl.DeviceIdType.MESH,
+    )
+
+
+def each_peer(action, part, rows, buffers):
+    def body(offset, carry):
+        action(peer_copy(offset, part, rows, *buffers))
+        return carry
+
+    lax.fori_loop(1, lax.axis_size("space"), body, 0)
+
+
+def start_part(part, rows, buffers):
+    each_peer(lambda copy: copy.start(), part, rows, buffers)
+    send, recv = buffers[:2]
+    me = lax.axis_index("space")
+    low, high = rows
+    recv[me, low:high, :] = send[me, low:high, :]
+
+
+def row_parts(padded):
+    tiles = padded // PAD_ROWS
+    cut = max(tiles * 2 // 5, 1)
+    parts = [(0, cut), (cut, tiles)] if cut < tiles else [(0, tiles)]
+    return parts
+
+
+def exchange_and_mix(to_owner, to_planes, mix_tile, out_ref):
+    padded = to_owner[0].shape[1]
+    parts = row_parts(padded)
+    rows = [(low * PAD_ROWS, high * PAD_ROWS) for low, high in parts]
+    for part in range(len(parts)):
+        start_part(part, rows[part], to_owner)
+    for part, (low, high) in enumerate(parts):
+        each_peer(lambda copy: copy.wait_recv(), part, rows[part], to_owner)
+        for tile in range(low, high):
+            mix_tile(tile)
+        start_part(part, rows[part], to_planes)
+    for part in range(len(parts)):
+        each_peer(lambda copy: copy.wait_recv(), part, rows[part], to_planes)
+    for part in range(len(parts)):
+        each_peer(lambda copy: copy.wait_send(), part, rows[part], to_owner)
+        each_peer(lambda copy: copy.wait_send(), part, rows[part], to_planes)
+    out_ref[...] = to_planes[1][...]
+
+
+def mix_one_tile(tile, in_ref, w_ref, tables, spectrum_ref, send_ref):
+    xf_ref, xb_ref, pick_ref, fold_ref = tables
+    own = w_ref.shape[0]
+    rows = PAD_ROWS * KX
+    first = tile * PAD_ROWS
+    pairs = min(PAD_ROWS, own - first)
+    if pairs <= 0:
+        send_ref[:, first : first + PAD_ROWS, :] = jnp.zeros(
+            (send_ref.shape[0], PAD_ROWS, send_ref.shape[2]), jnp.float32
+        )
+        return
+    spectrum = x_forward(in_ref, tile, xf_ref[...])
+    spectrum_ref[tile * rows : (tile + 1) * rows, :] = spectrum
+    mixed = mixed_rows(spectrum[: pairs * KX], w_ref, first, pairs, pick_ref, fold_ref)
+    x_backward(mixed, send_ref, tile, xb_ref[...])
+
+
+def repeat_matrix(lanes, channels):
+    row = lax.broadcasted_iota(jnp.int32, (lanes, channels), 0)
+    column = lax.broadcasted_iota(jnp.int32, (lanes, channels), 1)
+    return (row % channels == column).astype(jnp.float32).astype(jnp.bfloat16)
+
+
+def repeated_table(weight, lanes, flip):
+    channels = weight.shape[0]
+    repeat = repeat_matrix(lanes, channels)
+    inner = lax.dot_general(
+        repeat,
+        weight,
+        (((1,), (1 if flip else 0,)), ((), ())),
+        preferred_element_type=jnp.float32,
+    ).astype(jnp.bfloat16)
+    full = lax.dot_general(
+        inner, repeat, (((1,), (1,)), ((), ())), preferred_element_type=jnp.float32
+    )
+    row = lax.broadcasted_iota(jnp.int32, (lanes, lanes), 0)
+    lane = lax.broadcasted_iota(jnp.int32, (lanes, lanes), 1)
+    return jnp.where(row // channels == lane // channels, full, 0.0).astype(jnp.bfloat16)
+
+
+def spectrum_kernel(
+    count,
+    own,
+    f_ref,
+    zt_ref,
+    tt_ref,
+    yt_ref,
+    w_ref,
+    xf_ref,
+    xb_ref,
+    pick_ref,
+    fold_ref,
+    spectrum_ref,
+    out_ref,
+    zbuf,
+    spec,
+    send_a,
+    recv_a,
+    send_b,
+    recv_b,
+    send_sems_a,
+    recv_sems_a,
+    send_sems_b,
+    recv_sems_b,
+):
     step = pl.program_id(0)
+
+    @pl.when(step == 0)
+    def _():
+        greet_all()
+
     lanes = zbuf.shape[1]
     chunk = z_forward(lambda y: f_ref[y], count, zt_ref[...], tt_ref[...])
     zbuf[pl.ds(pl.multiple_of(step * (count * KZ), 8), count * KZ), :] = chunk
@@ -401,7 +546,15 @@
     @pl.when(step == pl.num_programs(0) - 1)
     def _():
         y_forward(zbuf, spec, yt_ref[...], zbuf.shape[0] // KZ, lanes)
-        write_blocks(spec, out_ref, own, jnp.zeros((1, lanes), jnp.float32))
+        write_blocks(spec, send_a, own, jnp.zeros((1, lanes), jnp.float32))
+        await_all()
+        tables = (xf_ref, xb_ref, pick_ref, fold_ref)
+        exchange_and_mix(
+            (send_a, recv_a, send_sems_a, recv_sems_a),
+            (send_b, recv_b, send_sems_b, recv_sems_b),
+            lambda tile: mix_one_tile(tile, recv_a, w_ref, tables, spectrum_ref, send_b),
+            out_ref,
+        )
 
 
 def activation_kernel(
@@ -420,14 +573,31 @@
     zt_ref,
     tt_ref,
     yt_ref,
+    w_ref,
+    xf_ref,
+    xb_ref,
+    pick_ref,
+    fold_ref,
     out_ref,
     grad_ref,
-    send_ref,
+    spectrum_ref,
+    arrived_ref,
+    stats_ref,
     ubuf,
     zbuf,
     spec,
     outer,
     total_row,
+    skip_table,
+    bias_buf,
+    send_a,
+    recv_a,
+    send_b,
+    recv_b,
+    send_sems_a,
+    recv_sems_a,
+    send_sems_b,
+    recv_sems_b,
 ):
     step = pl.program_id(0)
     lanes = ubuf.shape[1]
@@ -435,6 +605,14 @@
 
     @pl.when(step == 0)
     def _():
+        greet_all()
+        skip_table[...] = repeated_table(skip_ref[...], lanes, False)
+        bias_buf[...] = lax.dot_general(
+            bias_ref[...],
+            repeat_matrix(lanes, channels),
+            (((1,), (1,)), ((), ())),
+            preferred_element_type=jnp.float32,
+        )
         read_blocks(in_ref, spec, own, scale)
         y_backward(spec, ubuf, yb_ref[...], rows_y, lanes)
         outer[...] = jnp.zeros_like(outer)
@@ -442,10 +620,10 @@
 
     start = pl.multiple_of(step * (count * KZ), 8)
     pieces = z_backward(ubuf, start, count, tb_ref[...])
-    bias_row = bias_ref[...]
+    bias_row = bias_buf[...]
     for y in range(count):
         field = f_ref[y]
-        pre = dot32(zb_ref[...], pieces[y]) + dot32(field, skip_ref[...]) + bias_row
+        pre = dot32(zb_ref[...], pieces[y]) + dot32(field, skip_table[...]) + bias_row
         cdf = 0.5 * (1.0 + lax.erf(pre * (1.0 / math.sqrt(2.0))))
         pdf = jnp.exp(-0.5 * pre * pre) * (1.0 / math.sqrt(2.0 * math.pi))
         out_ref[y] = (pre * cdf).astype(jnp.bfloat16)
@@ -478,11 +656,36 @@
         group = lax.broadcasted_iota(jnp.int32, (1, lanes), 1) // channels
         bias_sum = jnp.sum(folded, axis=0, keepdims=True)
         bias_sum = jnp.where(group == channels, bias_sum, 0.0)
-        write_blocks(spec, send_ref, own, skip_row + bias_sum)
+        write_blocks(spec, send_a, own, skip_row + bias_sum)
+        await_all()
+        tables = (xf_ref, xb_ref, pick_ref, fold_ref)
+        exchange_and_mix(
+            (send_a, recv_a, send_sems_a, recv_sems_a),
+            (send_b, recv_b, send_sems_b, recv_sems_b),
+            lambda tile: mix_one_tile(tile, recv_a, w_ref, tables, spectrum_ref, send_b),
+            arrived_ref,
+        )
+        stats_ref[...] = jnp.sum(recv_a[:, own, :], axis=0, keepdims=True)
 
 
 def field_grad_kernel(
-    count, own, scale, in_ref, grad_ref, skip_ref, yb_ref, tb_ref, zb_ref, out_ref, ubuf, spec
+    count,
+    own,
+    scale,
+    root,
+    in_ref,
+    grad_ref,
+    skip_ref,
+    stats_ref,
+    yb_ref,
+    tb_ref,
+    zb_ref,
+    out_ref,
+    skip_out,
+    bias_out,
+    ubuf,
+    spec,
+    skip_table,
 ):
     step = pl.program_id(0)
     lanes = ubuf.shape[1]
@@ -491,11 +694,20 @@
     def _():
         read_blocks(in_ref, spec, own, scale)
         y_backward(spec, ubuf, yb_ref[...], ubuf.shape[0] // KZ, lanes)
+        skip_table[...] = repeated_table(skip_ref[...], lanes, True)
+        channels = skip_ref.shape[0]
+        group = lax.broadcasted_iota(jnp.int32, (2 * channels, lanes), 1) // channels
+        row = lax.broadcasted_iota(jnp.int32, (2 * channels, lanes), 0)
+        chosen = jnp.where(group == row, stats_ref[...] * root, 0.0)
+        fold = repeat_matrix(lanes, channels).astype(jnp.float32)
+        folded = jnp.dot(chosen, fold, precision=FULL_PRECISION)
+        skip_out[...] = folded[:channels]
+        bias_out[...] = folded[channels : channels + 1]
 
     start = pl.multiple_of(step * (count * KZ), 8)
     pieces = z_backward(ubuf, start, count, tb_ref[...])
     for y in range(count):
-        value = dot32(zb_ref[...], pieces[y]) + dot32(grad_ref[y], skip_ref[...])
+        value = dot32(zb_ref[...], pieces[y]) + dot32(grad_ref[y], skip_table[...])
         out_ref[y] = value.astype(jnp.bfloat16)
 
 
@@ -538,26 +750,6 @@
     return total
 
 
-def mix_kernel(with_stats, in_ref, w_ref, xf_ref, xb_ref, pick_ref, fold_ref, *outs):
-    spectrum_ref, send_ref = outs[:2]
-    own = w_ref.shape[0]
-    rows = PAD_ROWS * KX
-    for tile in range(pl.cdiv(own, PAD_ROWS)):
-        first = tile * PAD_ROWS
-        pairs = min(PAD_ROWS, own - first)
-        spectrum = x_forward(in_ref, tile, xf_ref[...])
-        spectrum_ref[tile * rows : (tile + 1) * rows, :] = spectrum
-        mixed = mixed_rows(spectrum[: pairs * KX], w_ref, first, pairs, pick_ref, fold_ref)
-        x_backward(mixed, send_ref, tile, xb_ref[...])
-    for tile in range(pl.cdiv(own, PAD_ROWS), in_ref.shape[1] // PAD_ROWS):
-        lanes = send_ref.shape[2]
-        send_ref[:, tile * PAD_ROWS : (tile + 1) * PAD_ROWS, :] = jnp.zeros(
-            (send_ref.shape[0], PAD_ROWS, lanes), jnp.float32
-        )
-    if with_stats:
-        outs[2][...] = jnp.sum(in_ref[:, own, :], axis=0, keepdims=True)
-
-
 def weight_gradient_kernel(scale, s_ref, t_ref, ps_ref, pt_ref, out_ref):
     pairs, _, _, wide = out_ref.shape
     for_s = jnp.concatenate(split_pair(s_ref[...]), axis=1)
@@ -570,7 +762,7 @@
 
 
 def whole(array):
-    zeros = (0,) * array.ndim
+    zeros = (0,) * len(array.shape)
     return pl.BlockSpec(array.shape, lambda *_: zeros)
 
 
@@ -596,10 +788,7 @@
     field = field.reshape(rows_y, rows_z, lanes)
     cotangent = cotangent.reshape(rows_y, rows_z, lanes)
     weights = spectral_weight.reshape(own, KT, KX, wide)
-    skip_f32 = skip_weight.astype(jnp.float32)
-    skip_table = block_diagonal(skip_f32, steps_t).astype(jnp.bfloat16)
-    skip_back = block_diagonal(skip_f32.T, steps_t).astype(jnp.bfloat16)
-    bias_row = jnp.tile(bias.astype(jnp.float32), steps_t).reshape(1, lanes)
+    bias_row = bias.reshape(1, channels)
     plane_spec = pl.BlockSpec((count, rows_z, lanes), lambda i: (i, 0, 0))
     plane_shape = jax.ShapeDtypeStruct((rows_y, rows_z, lanes), jnp.bfloat16)
     block_shape = jax.ShapeDtypeStruct((devices, padded, lanes), jnp.float32)
@@ -609,31 +798,29 @@
     plane_buf = pltpu.VMEM((rows_y * KZ, lanes), jnp.float32)
     spec_buf = pltpu.VMEM((KY * KZ, lanes), jnp.float32)
 
-    def exchange(blocks):
-        return lax.all_to_all(blocks, "space", split_axis=0, concat_axis=0, tiled=True)
-
-    operands = (field, t["z_fwd"], t["t_fwd"], t["y_fwd"])
-    sent = pl.pallas_call(
+    parts = len(row_parts(padded))
+    block_buf = pltpu.VMEM((devices, padded, lanes), jnp.float32)
+    sems = pltpu.SemaphoreType.DMA((parts, devices))
+    link_scratch = [block_buf] * 4 + [sems] * 4
+    spectrum_spec = pl.BlockSpec(spectrum_shape.shape, lambda *_: (0, 0))
+    mixing_s = (weights, t["x_fwd"], t["x_back"], t["pick_s"], t["fold_s"])
+    mixing_t = (weights, t["x_fwd"], t["x_back"], t["pick_t"], t["fold_t"])
+    operands = (field, t["z_fwd"], t["t_fwd"], t["y_fwd"]) + mixing_s
+    own_field, arrived = pl.pallas_call(
         functools.partial(spectrum_kernel, count, own),
         grid=(steps,),
         in_specs=[plane_spec] + [whole(x) for x in operands[1:]],
-        out_specs=block_spec,
-        out_shape=block_shape,
-        scratch_shapes=[plane_buf, spec_buf],
-        compiler_params=params(),
-        name="field_spectrum",
+        out_specs=[spectrum_spec, block_spec],
+        out_shape=[spectrum_shape, block_shape],
+        scratch_shapes=[plane_buf, spec_buf] + link_scratch,
+        compiler_params=params(collective_id=0, has_side_effects=True),
+        name="forward_mix",
     )(*operands)
-    own_field, sent = pl.pallas_call(
-        functools.partial(mix_kernel, False),
-        out_shape=[spectrum_shape, block_shape],
-        compiler_params=params(),
-        name="mix_forward",
-    )(exchange(sent), weights, t["x_fwd"], t["x_back"], t["pick_s"], t["fold_s"])
     operands = (
-        exchange(sent),
+        arrived,
         field,
         cotangent,
-        skip_table,
+        skip_weight,
         bias_row,
         t["y_back"],
         t["t_back"],
@@ -641,30 +828,27 @@
         t["z_fwd"],
         t["t_fwd"],
         t["y_fwd"],
-    )
-    output, grad_pre, sent = pl.pallas_call(
+    ) + mixing_t
+    stats_shape = jax.ShapeDtypeStruct((1, lanes), jnp.float32)
+    output, grad_pre, own_grad, arrived, stats = pl.pallas_call(
         functools.partial(activation_kernel, count, own, scale, channels),
         grid=(steps,),
         in_specs=[whole(operands[0]), plane_spec, plane_spec] + [whole(x) for x in operands[3:]],
-        out_specs=[plane_spec, plane_spec, block_spec],
-        out_shape=[plane_shape, plane_shape, block_shape],
+        out_specs=[plane_spec, plane_spec, spectrum_spec, block_spec, whole(stats_shape)],
+        out_shape=[plane_shape, plane_shape, spectrum_shape, block_shape, stats_shape],
         scratch_shapes=[
             plane_buf,
             plane_buf,
             spec_buf,
             pltpu.VMEM((lanes, lanes), jnp.float32),
             pltpu.VMEM((8, lanes), jnp.float32),
-        ],
-        compiler_params=params(),
-        name="activation",
+            pltpu.VMEM((lanes, lanes), jnp.bfloat16),
+            pltpu.VMEM((1, lanes), jnp.float32),
+        ]
+        + link_scratch,
+        compiler_params=params(collective_id=1, has_side_effects=True),
+        name="activation_mix",
     )(*operands)
-    own_grad, sent, stats = pl.pallas_call(
-        functools.partial(mix_kernel, True),
-        out_shape=[spectrum_shape, block_shape, jax.ShapeDtypeStruct((1, lanes), jnp.float32)],
-        compiler_params=params(),
-        name="mix_adjoint",
-    )(exchange(sent), weights, t["x_fwd"], t["x_back"], t["pick_t"], t["fold_t"])
-    arrived = exchange(sent)
     pairs = 4 if own % 4 == 0 else 1
     mode_spec = pl.BlockSpec((pairs * KX, lanes), lambda i: (i, 0))
     spectral_grad = pl.pallas_call(
@@ -679,27 +863,26 @@
         ),
         name="weight_gradient",
     )(own_field, own_grad, t["pick_s"], t["pick_t"])
-    operands = (arrived, grad_pre, skip_back, t["y_back"], t["t_back"], t["z_back"])
-    field_grad = pl.pallas_call(
-        functools.partial(field_grad_kernel, count, own, scale),
+    operands = (arrived, grad_pre, skip_weight, stats, t["y_back"], t["t_back"], t["z_back"])
+    root = 1.0 / math.sqrt(total)
+    square_shape = jax.ShapeDtypeStruct((channels, channels), jnp.float32)
+    line_shape = jax.ShapeDtypeStruct((1, channels), jnp.float32)
+    field_grad, skip_grad, bias_grad = pl.pallas_call(
+        functools.partial(field_grad_kernel, count, own, scale, root),
         grid=(steps,),
         in_specs=[whole(operands[0]), plane_spec] + [whole(x) for x in operands[2:]],
-        out_specs=plane_spec,
-        out_shape=plane_shape,
-        scratch_shapes=[plane_buf, spec_buf],
+        out_specs=[plane_spec, whole(square_shape), whole(line_shape)],
+        out_shape=[plane_shape, square_shape, line_shape],
+        scratch_shapes=[plane_buf, spec_buf, pltpu.VMEM((lanes, lanes), jnp.bfloat16)],
         compiler_params=params(),
         name="field_grad",
     )(*operands)
-    root = 1.0 / math.sqrt(total)
-    square = channels * channels
-    skip_grad = stats[0, :square].reshape(channels, channels) * root
-    bias_grad = stats[0, square : square + channels] * root
     return (
         output[None],
         field_grad[None],
         spectral_grad.reshape(own * KT, KX, wide),
         skip_grad,
-        bias_grad,
+        bias_grad.reshape(channels),
     )
 
 

time: 104 us -> 83 us (0.80)
  Pallas kernels: 38.5 us -> 71.3 us
  blocking collectives: 32.4 us -> 0 us
  waiting for transfers between devices: 8.15 us -> 0 us
  starting transfers between devices: 7.08 us -> 0 us
  local copies, waits for them, and re-layouts: 14.7 us -> 10.3 us
  other arithmetic: 1.82 us -> 0 us
    all_to_all x2 -> x0, blocking collectives: 32.4 us -> none  [exchange(): lax.all_to_all(blocks, 'space', split_axis=0, concat_axis=0, tiled=True)]
    pallas_call x1, Pallas kernels: 2.7 us -> 27.6 us  [fast_device(): pl.pallas_call(functools.partial(spectrum_kernel, count, own), grid=(step...]
    pallas_call x1, Pallas kernels: 10.3 us -> 32.4 us  [fast_device(): pl.pallas_call(functools.partial(activation_kernel, count, own, scale, ch...]
    pallas_call x3 -> x1, Pallas kernels: 19.4 us -> 5.22 us  [fast_device(): pl.pallas_call(functools.partial(field_grad_kernel, count, own, scale, ro...]
    all_to_all x2 -> x0, waiting for transfers between devices: 8.15 us -> none  [exchange(): lax.all_to_all(blocks, 'space', split_axis=0, concat_axis=0, tiled=True)]
    all_to_all x2 -> x0, starting transfers between devices: 7.08 us -> none  [exchange(): lax.all_to_all(blocks, 'space', split_axis=0, concat_axis=0, tiled=True)]
    convert_element_type x2 -> x0, local copies, waits for them, and re-layouts: 2.02 us -> none  [the longest x1 1.5 us: fast_device(): skip_table = block_diagonal(skip_f32, steps_t).astype(jnp.bfloat16)]
    unnamed x56 -> x35, local copies, waits for them, and re-layouts: 11.8 us -> 10.3 us
  transfers between devices with their start and end apart: 2 -> 0, of which waited for: 1 -> 0; matrix products, arithmetic and copies ran while one was open for 5% -> 0% of each run, Pallas kernels for 6% -> 0%
where the time goes in v1:
time: 83 us; the launch traced here: 82.3 us
  Pallas kernels  71.3 us (86%)
  local copies, waits for them, and re-layouts  10.3 us (12%)
    pallas_call x1, Pallas kernels, fast_device(): pl.pallas_call(functools.partial(activation_kernel, count, own, scale, ch...  32.4 us
    pallas_call x1, Pallas kernels, fast_device(): pl.pallas_call(functools.partial(spectrum_kernel, count, own), grid=(step...  27.6 us
    unnamed x35, local copies, waits for them, and re-layouts  10.3 us
    pallas_call x1, Pallas kernels, fast_device(): pl.pallas_call(functools.partial(weight_gradient_kernel, scale), grid=(ow...  6.1 us
    pallas_call x1, Pallas kernels, fast_device(): pl.pallas_call(functools.partial(field_grad_kernel, count, own, scale, ro...  5.22 us

profile of v1, /device:TPU:0, one launch (start us, length us, event | category | flops | bytes accessed | tf_op | source)
XLA Modules:
  0.0 82.3 jit_solution(16730228646514697843)
XLA Ops:
  0.6 0.0 copy-start
  0.6 1.5 %copy-done = bf16[288,24,128]{2,1,0:T(8,128)(2,1)S(1)} copy-done((bf16[288,24,128]{2,1,0:T(8,128)(2,1)S(1)}, bf16[288,24,128]{2,1,0:T(8,128)(2,1)}, u32[]{:S(2)}) %copy-start) | copy-done | bytes 1769496
  2.1 0.0 copy-start.2
  2.1 1.0 %copy-done.2 = bf16[384,384]{1,0:T(8,128)(2,1)S(1)} copy-done((bf16[384,384]{1,0:T(8,128)(2,1)S(1)}, bf16[384,384]{1,0:T(8,128)(2,1)}, u32[]{:S(2)}) %copy-start.2) | copy-done | bytes 294936
  3.1 0.0 copy-start.4
  3.1 1.2 %copy-done.4 = bf16[8,256,256]{2,1,0:T(8,128)(2,1)S(1)} copy-done((bf16[8,256,256]{2,1,0:T(8,128)(2,1)S(1)}, bf16[8,256,256]{2,1,0:T(8,128)(2,1)}, u32[]{:S(2)}) %copy-start.4) | copy-done | bytes 1048600
  4.3 0.0 copy-start.6
  4.3 0.9 %copy-done.6 = bf16[256,384]{1,0:T(8,128)(2,1)S(1)} copy-done((bf16[256,384]{1,0:T(8,128)(2,1)S(1)}, bf16[256,384]{1,0:T(8,128)(2,1)}, u32[]{:S(2)}) %copy-start.6) | copy-done | bytes 196632
  5.2 0.0 copy-start.8
  5.2 1.0 %copy-done.8 = bf16[8,256,128]{2,1,0:T(8,128)(2,1)S(1)} copy-done((bf16[8,256,128]{2,1,0:T(8,128)(2,1)S(1)}, bf16[8,256,128]{2,1,0:T(8,128)(2,1)}, u32[]{:S(2)}) %copy-start.8) | copy-done | bytes 524312
  6.3 0.0 copy-start.9
  6.3 0.8 %copy-done.9 = bf16[256,128]{1,0:T(8,128)(2,1)S(1)} copy-done((bf16[256,128]{1,0:T(8,128)(2,1)S(1)}, bf16[256,128]{1,0:T(8,128)(2,1)}, u32[]{:S(2)}) %copy-start.9) | copy-done | bytes 65560
  7.1 0.0 copy-start.11
  7.1 0.7 copy-done.11
  7.8 0.0 copy-start.3
  7.8 0.0 copy-start.7
  7.8 0.0 copy-start.10
  7.8 0.0 copy-start.12
  7.8 0.0 copy-start.13
  7.8 0.0 copy-start.14
  7.8 0.0 copy-start.15
  7.9 27.6 %forward_mix.1 = (f32[960,128]{1,0:T(8,128)S(1)}, f32[16,40,128]{2,1,0:T(8,128)S(1)}) custom-call(bf16[96,96,128]{2,1,0:T(8,128)(2,1)} %bitcast.11, bf16[48,96]{1,0:T(8,128)(2,1)S(1)} %copy-done.11, bf16[256,128]{1,0:T(8,128)(2,1)S(1)} %copy-done.9, bf16[48,96]{1,0:T(8,128)(2,1)S(1)} %copy-done.11, bf16[36,8,24,128]{3,2,1,0:T(8,128)(2,1)S(1)} %bitcast.8, ...), custom_call_target="tpu_custom_call" | custom-call | tf_op jit(solution)/shard_map/forward_mix/pallas_call | solution.py:809
  35.4 0.0 copy-done.3
  35.5 0.0 copy-done.7
  35.5 0.0 copy-done.10
  35.5 0.0 copy-done.12
  35.5 0.0 copy-done.13
  35.5 0.0 copy-done.14
  35.5 0.0 copy-done.15
  35.5 0.0 copy-start.5
  35.5 32.4 %activation_mix.1 = (bf16[96,96,128]{2,1,0:T(8,128)(2,1)}, bf16[96,96,128]{2,1,0:T(8,128)(2,1)}, f32[960,128]{1,0:T(8,128)S(1)}, f32[16,40,128]{2,1,0:T(8,128)S(1)}, f32[1,128]{1,0:T(1,128)S(1)}) custom-call(f32[16,40,128]{2,1,0:T(8,128)S(1)} %get-tuple-element.15.in_ref, bf16[96,96,128]{2,1,0:T(8,128)(2,1)} %bitcast.12, bf16[96,96,128]{2,1,0:T(8,128)(2,1)} %bitcast.13, ...), custom_call_target="tpu_custom_call" | custom-call | tf_op jit(solution)/shard_map/activation_mix/pallas_call | solution.py:833
  67.9 0.0 copy-start.1
  67.9 1.7 %copy-done.1 = bf16[96,96,128]{2,1,0:T(8,128)(2,1)S(1)} copy-done((bf16[96,96,128]{2,1,0:T(8,128)(2,1)S(1)}, bf16[96,96,128]{2,1,0:T(8,128)(2,1)}, u32[]{:S(2)}) %copy-start.1) | copy-done | bytes 2359320
  69.6 5.2 %field_grad.1 = (bf16[96,96,128]{2,1,0:T(8,128)(2,1)}, f32[8,8]{1,0:T(8,128)}, f32[1,8]{1,0:T(1,128)}) custom-call(f32[16,40,128]{2,1,0:T(8,128)S(1)} %get-tuple-element.17.in_ref, bf16[96,96,128]{2,1,0:T(8,128)(2,1)S(1)} %copy-done.1, bf16[8,8]{1,0:T(8,128)(2,1)S(1)} %copy-done.14, f32[1,128]{1,0:T(1,128)S(1)} %get-tuple-element.19.stats_ref, ...), custom_call_target="tpu_custom_call" | custom-call | tf_op jit(solution)/shard_map/field_grad/pallas_call | solution.py:870
  74.8 0.0 copy-done.5
  74.8 0.0 copy-start.16
  74.8 6.1 %weight_gradient.1 = f32[36,8,24,128]{3,2,1,0:T(8,128)} custom-call(f32[960,128]{1,0:T(8,128)S(1)} %get-tuple-element.21.s_ref, f32[960,128]{1,0:T(8,128)S(1)} %get-tuple-element.22.t_ref, bf16[8,256,256]{2,1,0:T(8,128)(2,1)S(1)} %copy-done.5, bf16[8,256,256]{2,1,0:T(8,128)(2,1)S(1)} %copy-done.3), custom_call_target="tpu_custom_call" | custom-call | flops 1811939328 | bytes 7077888 | tf_op jit(solution)/shard_map/weight_gradient/pallas_call | solution.py:854
  80.9 0.0 copy-done.16
  80.9 1.4 %copy.23 = bf16[1,96,96,128]{3,2,1,0:T(8,128)(2,1)} copy(bf16[1,96,96,128]{3,2,1,0:T(8,128)(2,1)S(1)} %bitcast.14) | data formatting | bytes 4718592
Async XLA Ops:
  0.6 1.5 %copy-start = (bf16[288,24,128]{2,1,0:T(8,128)(2,1)S(1)}, bf16[288,24,128]{2,1,0:T(8,128)(2,1)}, u32[]{:S(2)}) copy-start(bf16[288,24,128]{2,1,0:T(8,128)(2,1)} %param.19) | copy-start | bytes 5308420
  2.1 1.0 %copy-start.2 = (bf16[384,384]{1,0:T(8,128)(2,1)S(1)}, bf16[384,384]{1,0:T(8,128)(2,1)}, u32[]{:S(2)}) copy-start(bf16[384,384]{1,0:T(8,128)(2,1)} %constant.27.clone.xf_ref) | copy-start | bytes 884740
  3.1 1.2 %copy-start.4 = (bf16[8,256,256]{2,1,0:T(8,128)(2,1)S(1)}, bf16[8,256,256]{2,1,0:T(8,128)(2,1)}, u32[]{:S(2)}) copy-start(bf16[8,256,256]{2,1,0:T(8,128)(2,1)} %constant.29.clone.pick_ref.ps_ref) | copy-start | bytes 3145732
  4.3 0.9 %copy-start.6 = (bf16[256,384]{1,0:T(8,128)(2,1)S(1)}, bf16[256,384]{1,0:T(8,128)(2,1)}, u32[]{:S(2)}) copy-start(bf16[256,384]{1,0:T(8,128)(2,1)} %constant.28.clone.xb_ref) | copy-start | bytes 589828
  5.2 1.0 %copy-start.8 = (bf16[8,256,128]{2,1,0:T(8,128)(2,1)S(1)}, bf16[8,256,128]{2,1,0:T(8,128)(2,1)}, u32[]{:S(2)}) copy-start(bf16[8,256,128]{2,1,0:T(8,128)(2,1)} %constant.31.clone.fold_ref) | copy-start | bytes 1572868
  6.3 0.8 %copy-start.9 = (bf16[256,128]{1,0:T(8,128)(2,1)S(1)}, bf16[256,128]{1,0:T(8,128)(2,1)}, u32[]{:S(2)}) copy-start(bf16[256,128]{1,0:T(8,128)(2,1)} %constant.23.clone.tt_ref) | copy-start | bytes 196612
  7.1 0.7 copy-start.11
  7.8 27.6 %copy-start.3 = (bf16[8,256,256]{2,1,0:T(8,128)(2,1)S(1)}, bf16[8,256,256]{2,1,0:T(8,128)(2,1)}, u32[]{:S(2)}) copy-start(bf16[8,256,256]{2,1,0:T(8,128)(2,1)} %constant.30.clone.pick_ref.pt_ref) | copy-start | bytes 3145732
  7.8 27.6 %copy-start.7 = (bf16[8,256,128]{2,1,0:T(8,128)(2,1)S(1)}, bf16[8,256,128]{2,1,0:T(8,128)(2,1)}, u32[]{:S(2)}) copy-start(bf16[8,256,128]{2,1,0:T(8,128)(2,1)} %constant.32.clone.fold_ref) | copy-start | bytes 1572868
  7.8 27.6 %copy-start.10 = (bf16[128,256]{1,0:T(8,128)(2,1)S(1)}, bf16[128,256]{1,0:T(8,128)(2,1)}, u32[]{:S(2)}) copy-start(bf16[128,256]{1,0:T(8,128)(2,1)} %constant.25.clone.tb_ref) | copy-start | bytes 196612
  7.8 27.7 %copy-start.12 = (bf16[96,144]{1,0:T(8,128)(2,1)S(1)}, bf16[96,144]{1,0:T(8,128)(2,1)}, u32[]{:S(2)}) copy-start(bf16[96,144]{1,0:T(8,128)(2,1)} %constant.24.clone.yb_ref) | copy-start | bytes 82948
  7.8 27.7 %copy-start.13 = (bf16[96,48]{1,0:T(8,128)(2,1)S(1)}, bf16[96,48]{1,0:T(8,128)(2,1)}, u32[]{:S(2)}) copy-start(bf16[96,48]{1,0:T(8,128)(2,1)} %constant.26.clone.zb_ref) | copy-start | bytes 27652
  7.8 27.7 %copy-start.14 = (bf16[8,8]{1,0:T(8,128)(2,1)S(1)}, bf16[8,8]{1,0:T(8,128)(2,1)}, u32[]{:S(2)}) copy-start(bf16[8,8]{1,0:T(8,128)(2,1)} %skip_ref.3) | copy-start | bytes 388
  7.8 27.7 %copy-start.15 = (bf16[8]{0:T(256)(128)(2,1)S(1)}, bf16[8]{0:T(256)(128)(2,1)}, u32[]{:S(2)}) copy-start(bf16[8]{0:T(256)(128)(2,1)} %param.21) | copy-start | bytes 52
  35.5 39.3 %copy-start.5 = (bf16[8,256,256]{2,1,0:T(8,128)(2,1)S(1)}, bf16[8,256,256]{2,1,0:T(8,128)(2,1)}, u32[]{:S(2)}) copy-start(bf16[8,256,256]{2,1,0:T(8,128)(2,1)} %constant.29.clone.pick_ref.ps_ref) | copy-start | bytes 3145732
  67.9 1.7 %copy-start.1 = (bf16[96,96,128]{2,1,0:T(8,128)(2,1)S(1)}, bf16[96,96,128]{2,1,0:T(8,128)(2,1)}, u32[]{:S(2)}) copy-start(bf16[96,96,128]{2,1,0:T(8,128)(2,1)} %get-tuple-element.18.grad_ref) | copy-start | bytes 7077892
  74.8 6.1 %copy-start.16 = (bf16[96,96,128]{2,1,0:T(8,128)(2,1)S(1)}, bf16[96,96,128]{2,1,0:T(8,128)(2,1)}, u32[]{:S(2)}) copy-start(bf16[96,96,128]{2,1,0:T(8,128)(2,1)} %get-tuple-element.16) | copy-start | bytes 7077892

commit v2 on v1

--- a/solution.py
+++ b/solution.py
@@ -468,6 +468,13 @@
     out_ref[...] = to_planes[1][...]
 
 
+def fetch(sources, targets, sems):
+    return [
+        pltpu.make_async_copy(source, target, sems.at[index])
+        for index, (source, target) in enumerate(zip(sources, targets))
+    ]
+
+
 def mix_one_tile(tile, in_ref, w_ref, tables, spectrum_ref, send_ref):
     xf_ref, xb_ref, pick_ref, fold_ref = tables
     own = w_ref.shape[0]
@@ -515,11 +522,11 @@
     zt_ref,
     tt_ref,
     yt_ref,
-    w_ref,
+    w_hbm,
     xf_ref,
     xb_ref,
-    pick_ref,
-    fold_ref,
+    pick_hbm,
+    fold_hbm,
     spectrum_ref,
     out_ref,
     zbuf,
@@ -532,12 +539,19 @@
     recv_sems_a,
     send_sems_b,
     recv_sems_b,
+    w_ref,
+    pick_ref,
+    fold_ref,
+    fetch_sems,
 ):
     step = pl.program_id(0)
+    fetches = fetch((w_hbm, pick_hbm, fold_hbm), (w_ref, pick_ref, fold_ref), fetch_sems)
 
     @pl.when(step == 0)
     def _():
         greet_all()
+        for copy in fetches:
+            copy.start()
 
     lanes = zbuf.shape[1]
     chunk = z_forward(lambda y: f_ref[y], count, zt_ref[...], tt_ref[...])
@@ -548,6 +562,8 @@
         y_forward(zbuf, spec, yt_ref[...], zbuf.shape[0] // KZ, lanes)
         write_blocks(spec, send_a, own, jnp.zeros((1, lanes), jnp.float32))
         await_all()
+        for copy in fetches:
+            copy.wait()
         tables = (xf_ref, xb_ref, pick_ref, fold_ref)
         exchange_and_mix(
             (send_a, recv_a, send_sems_a, recv_sems_a),
@@ -573,11 +589,11 @@
     zt_ref,
     tt_ref,
     yt_ref,
-    w_ref,
+    w_hbm,
     xf_ref,
     xb_ref,
-    pick_ref,
-    fold_ref,
+    pick_hbm,
+    fold_hbm,
     out_ref,
     grad_ref,
     spectrum_ref,
@@ -598,14 +614,21 @@
     recv_sems_a,
     send_sems_b,
     recv_sems_b,
+    w_ref,
+    pick_ref,
+    fold_ref,
+    fetch_sems,
 ):
     step = pl.program_id(0)
+    fetches = fetch((w_hbm, pick_hbm, fold_hbm), (w_ref, pick_ref, fold_ref), fetch_sems)
     lanes = ubuf.shape[1]
     rows_y = ubuf.shape[0] // KZ
 
     @pl.when(step == 0)
     def _():
         greet_all()
+        for copy in fetches:
+            copy.start()
         skip_table[...] = repeated_table(skip_ref[...], lanes, False)
         bias_buf[...] = lax.dot_general(
             bias_ref[...],
@@ -658,6 +681,8 @@
         bias_sum = jnp.where(group == channels, bias_sum, 0.0)
         write_blocks(spec, send_a, own, skip_row + bias_sum)
         await_all()
+        for copy in fetches:
+            copy.wait()
         tables = (xf_ref, xb_ref, pick_ref, fold_ref)
         exchange_and_mix(
             (send_a, recv_a, send_sems_a, recv_sems_a),
@@ -766,8 +791,8 @@
     return pl.BlockSpec(array.shape, lambda *_: zeros)
 
 
-def params(**extra):
-    return pltpu.CompilerParams(vmem_limit_bytes=48 * 1024 * 1024, **extra)
+def params(mebibytes, **extra):
+    return pltpu.CompilerParams(vmem_limit_bytes=mebibytes * 1024 * 1024, **extra)
 
 
 def fast_device(field, cotangent, spectral_weight, skip_weight, bias):
@@ -781,7 +806,7 @@
     padded = (own // PAD_ROWS + 1) * PAD_ROWS
     wide = spectral_weight.shape[2]
     t = make_tables(rows_y, rows_z, steps_t, channels, devices)
-    count = 16
+    count = 32
     while rows_y % count:
         count //= 2
     steps = rows_y // count
@@ -802,6 +827,12 @@
     block_buf = pltpu.VMEM((devices, padded, lanes), jnp.float32)
     sems = pltpu.SemaphoreType.DMA((parts, devices))
     link_scratch = [block_buf] * 4 + [sems] * 4
+    link_scratch += [
+        pltpu.VMEM(x.shape, x.dtype) for x in (weights, t["pick_s"], t["fold_s"])
+    ]
+    link_scratch += [pltpu.SemaphoreType.DMA((3,))]
+    far = pl.BlockSpec(memory_space=pl.ANY)
+    mixing_specs = [far, whole(t["x_fwd"]), whole(t["x_back"]), far, far]
     spectrum_spec = pl.BlockSpec(spectrum_shape.shape, lambda *_: (0, 0))
     mixing_s = (weights, t["x_fwd"], t["x_back"], t["pick_s"], t["fold_s"])
     mixing_t = (weights, t["x_fwd"], t["x_back"], t["pick_t"], t["fold_t"])
@@ -809,11 +840,11 @@
     own_field, arrived = pl.pallas_call(
         functools.partial(spectrum_kernel, count, own),
         grid=(steps,),
-        in_specs=[plane_spec] + [whole(x) for x in operands[1:]],
+        in_specs=[plane_spec] + [whole(x) for x in operands[1:-5]] + mixing_specs,
         out_specs=[spectrum_spec, block_spec],
         out_shape=[spectrum_shape, block_shape],
         scratch_shapes=[plane_buf, spec_buf] + link_scratch,
-        compiler_params=params(collective_id=0, has_side_effects=True),
+        compiler_params=params(60, collective_id=0, has_side_effects=True),
         name="forward_mix",
     )(*operands)
     operands = (
@@ -833,7 +864,9 @@
     output, grad_pre, own_grad, arrived, stats = pl.pallas_call(
         functools.partial(activation_kernel, count, own, scale, channels),
         grid=(steps,),
-        in_specs=[whole(operands[0]), plane_spec, plane_spec] + [whole(x) for x in operands[3:]],
+        in_specs=[whole(operands[0]), plane_spec, plane_spec]
+        + [whole(x) for x in operands[3:-5]]
+        + mixing_specs,
         out_specs=[plane_spec, plane_spec, spectrum_spec, block_spec, whole(stats_shape)],
         out_shape=[plane_shape, plane_shape, spectrum_shape, block_shape, stats_shape],
         scratch_shapes=[
@@ -846,10 +879,10 @@
             pltpu.VMEM((1, lanes), jnp.float32),
         ]
         + link_scratch,
-        compiler_params=params(collective_id=1, has_side_effects=True),
+        compiler_params=params(60, collective_id=1, has_side_effects=True),
         name="activation_mix",
     )(*operands)
-    pairs = 4 if own % 4 == 0 else 1
+    pairs = 12 if own % 12 == 0 else 1
     mode_spec = pl.BlockSpec((pairs * KX, lanes), lambda i: (i, 0))
     spectral_grad = pl.pallas_call(
         functools.partial(weight_gradient_kernel, scale),
@@ -857,7 +890,7 @@
         in_specs=[mode_spec, mode_spec, whole(t["pick_s"]), whole(t["pick_t"])],
         out_specs=pl.BlockSpec((pairs, KT, KX, wide), lambda i: (i, 0, 0, 0)),
         out_shape=jax.ShapeDtypeStruct((own, KT, KX, wide), jnp.float32),
-        compiler_params=params(),
+        compiler_params=params(48),
         cost_estimate=pl.CostEstimate(
             flops=4 * own * KX * KT * 65536, bytes_accessed=8 * own * KX * KT * wide, transcendentals=0
         ),
@@ -874,7 +907,7 @@
         out_specs=[plane_spec, whole(square_shape), whole(line_shape)],
         out_shape=[plane_shape, square_shape, line_shape],
         scratch_shapes=[plane_buf, spec_buf, pltpu.VMEM((lanes, lanes), jnp.bfloat16)],
-        compiler_params=params(),
+        compiler_params=params(48),
         name="field_grad",
     )(*operands)
     return (

time: 83 us -> 73.4 us (0.88)
  local copies, waits for them, and re-layouts: 10.3 us -> 4.71 us
  Pallas kernels: 71.3 us -> 67.6 us
    unnamed x35 -> x25, local copies, waits for them, and re-layouts: 10.3 us -> 4.71 us
    pallas_call x1, Pallas kernels: 6.1 us -> 3.63 us  [fast_device(): pl.pallas_call(functools.partial(weight_gradient_kernel, scale), grid=(ow...]
    pallas_call x1, Pallas kernels: 5.22 us -> 4.08 us  [fast_device(): pl.pallas_call(functools.partial(field_grad_kernel, count, own, scale, ro...]
where the time goes in v2:
time: 73.4 us; the launch traced here: 73.1 us
  Pallas kernels  67.6 us (92%)
  local copies, waits for them, and re-layouts  4.71 us (6%)
  between operations  0.77 us (1%)
    pallas_call x1, Pallas kernels, fast_device(): pl.pallas_call(functools.partial(activation_kernel, count, own, scale, ch...  32 us
    pallas_call x1, Pallas kernels, fast_device(): pl.pallas_call(functools.partial(spectrum_kernel, count, own), grid=(step...  27.8 us
    unnamed x25, local copies, waits for them, and re-layouts  4.71 us
    pallas_call x1, Pallas kernels, fast_device(): pl.pallas_call(functools.partial(field_grad_kernel, count, own, scale, ro...  4.08 us
    pallas_call x1, Pallas kernels, fast_device(): pl.pallas_call(functools.partial(weight_gradient_kernel, scale), grid=(ow...  3.63 us

profile of v2, /device:TPU:0, one launch (start us, length us, event | category | flops | bytes accessed | tf_op | source)
XLA Modules:
  0.0 73.1 jit_solution(615488028357425489)
XLA Ops:
  0.6 27.8 %forward_mix.1 = (f32[960,128]{1,0:T(8,128)}, f32[16,40,128]{2,1,0:T(8,128)}) custom-call(bf16[96,96,128]{2,1,0:T(8,128)(2,1)} %bitcast.8, bf16[48,96]{1,0:T(8,128)(2,1)} %constant.22.clone.zt_ref.yt_ref, bf16[256,128]{1,0:T(8,128)(2,1)} %constant.23.clone.tt_ref, bf16[48,96]{1,0:T(8,128)(2,1)} %constant.22.clone.zt_ref.yt_ref, ...), custom_call_target="tpu_custom_call" | custom-call | tf_op jit(solution)/shard_map/forward_mix/pallas_call | solution.py:840
  28.5 0.0 copy-start.4
  28.5 0.0 copy-start.5
  28.5 0.0 copy-start.6
  28.5 0.0 copy-start.7
  28.5 0.0 copy-start.1
  28.5 0.0 copy-start.2
  28.6 0.0 copy-start.9
  28.6 32.0 %activation_mix.1 = (bf16[96,96,128]{2,1,0:T(8,128)(2,1)}, bf16[96,96,128]{2,1,0:T(8,128)(2,1)}, f32[960,128]{1,0:T(8,128)}, f32[16,40,128]{2,1,0:T(8,128)}, f32[1,128]{1,0:T(1,128)}) custom-call(f32[16,40,128]{2,1,0:T(8,128)} %get-tuple-element.15.in_ref, bf16[96,96,128]{2,1,0:T(8,128)(2,1)} %bitcast.9, bf16[96,96,128]{2,1,0:T(8,128)(2,1)} %bitcast.12, ...), custom_call_target="tpu_custom_call" | custom-call | tf_op jit(solution)/shard_map/activation_mix/pallas_call | solution.py:864
  60.6 0.0 copy-done.4
  60.6 0.0 copy-done.5
  60.6 0.0 copy-done.6
  60.6 0.0 copy-done.7
  60.6 0.0 copy-start
  60.7 1.7 %copy-done = bf16[96,96,128]{2,1,0:T(8,128)(2,1)S(1)} copy-done((bf16[96,96,128]{2,1,0:T(8,128)(2,1)S(1)}, bf16[96,96,128]{2,1,0:T(8,128)(2,1)}, u32[]{:S(2)}) %copy-start) | copy-done | bytes 2359320
  62.3 0.0 copy-start.3
  62.3 1.0 %copy-done.3 = f32[16,40,128]{2,1,0:T(8,128)S(1)} copy-done((f32[16,40,128]{2,1,0:T(8,128)S(1)}, f32[16,40,128]{2,1,0:T(8,128)}, u32[]{:S(2)}) %copy-start.3) | copy-done | bytes 327704
  63.3 0.0 copy-start.8
  63.3 0.6 copy-done.8
  63.9 0.0 copy-start.10
  63.9 4.1 %field_grad.1 = (bf16[96,96,128]{2,1,0:T(8,128)(2,1)}, f32[8,8]{1,0:T(8,128)}, f32[1,8]{1,0:T(1,128)}) custom-call(f32[16,40,128]{2,1,0:T(8,128)S(1)} %copy-done.3, bf16[96,96,128]{2,1,0:T(8,128)(2,1)S(1)} %copy-done, bf16[8,8]{1,0:T(8,128)(2,1)S(1)} %copy-done.7, f32[1,128]{1,0:T(1,128)S(1)} %copy-done.8, bf16[96,144]{1,0:T(8,128)(2,1)S(1)} %copy-done.5, ...), custom_call_target="tpu_custom_call" | custom-call | tf_op jit(solution)/shard_map/field_grad/pallas_call | solution.py:903
  68.0 0.0 copy-done.1
  68.0 0.0 copy-done.2
  68.0 0.0 copy-done.9
  68.0 0.0 copy-done.10
  68.0 0.0 copy-start.11
  68.0 3.6 %weight_gradient.1 = f32[36,8,24,128]{3,2,1,0:T(8,128)} custom-call(f32[960,128]{1,0:T(8,128)S(1)} %copy-done.9, f32[960,128]{1,0:T(8,128)S(1)} %copy-done.10, bf16[8,256,256]{2,1,0:T(8,128)(2,1)S(1)} %copy-done.2, bf16[8,256,256]{2,1,0:T(8,128)(2,1)S(1)} %copy-done.1), custom_call_target="tpu_custom_call" | custom-call | flops 1811939328 | bytes 7077888 | tf_op jit(solution)/shard_map/weight_gradient/pallas_call | solution.py:887
  71.6 0.0 copy-done.11
  71.6 1.4 %copy.23 = bf16[1,96,96,128]{3,2,1,0:T(8,128)(2,1)} copy(bf16[1,96,96,128]{3,2,1,0:T(8,128)(2,1)S(1)} %bitcast.13) | data formatting | bytes 4718592
Async XLA Ops:
  28.5 32.1 %copy-start.4 = (bf16[128,256]{1,0:T(8,128)(2,1)S(1)}, bf16[128,256]{1,0:T(8,128)(2,1)}, u32[]{:S(2)}) copy-start(bf16[128,256]{1,0:T(8,128)(2,1)} %constant.25.clone.tb_ref) | copy-start | bytes 196612
  28.5 32.1 %copy-start.5 = (bf16[96,144]{1,0:T(8,128)(2,1)S(1)}, bf16[96,144]{1,0:T(8,128)(2,1)}, u32[]{:S(2)}) copy-start(bf16[96,144]{1,0:T(8,128)(2,1)} %constant.24.clone.yb_ref) | copy-start | bytes 82948
  28.5 32.1 %copy-start.6 = (bf16[96,48]{1,0:T(8,128)(2,1)S(1)}, bf16[96,48]{1,0:T(8,128)(2,1)}, u32[]{:S(2)}) copy-start(bf16[96,48]{1,0:T(8,128)(2,1)} %constant.26.clone.zb_ref) | copy-start | bytes 27652
  28.5 32.1 %copy-start.7 = (bf16[8,8]{1,0:T(8,128)(2,1)S(1)}, bf16[8,8]{1,0:T(8,128)(2,1)}, u32[]{:S(2)}) copy-start(bf16[8,8]{1,0:T(8,128)(2,1)} %skip_ref.3) | copy-start | bytes 388
  28.5 39.5 %copy-start.1 = (bf16[8,256,256]{2,1,0:T(8,128)(2,1)S(1)}, bf16[8,256,256]{2,1,0:T(8,128)(2,1)}, u32[]{:S(2)}) copy-start(bf16[8,256,256]{2,1,0:T(8,128)(2,1)} %constant.30.clone.pick_hbm.pt_ref) | copy-start | bytes 3145732
  28.5 39.4 %copy-start.2 = (bf16[8,256,256]{2,1,0:T(8,128)(2,1)S(1)}, bf16[8,256,256]{2,1,0:T(8,128)(2,1)}, u32[]{:S(2)}) copy-start(bf16[8,256,256]{2,1,0:T(8,128)(2,1)} %constant.29.clone.pick_hbm.ps_ref) | copy-start | bytes 3145732
  28.6 39.4 %copy-start.9 = (f32[960,128]{1,0:T(8,128)S(1)}, f32[960,128]{1,0:T(8,128)}, u32[]{:S(2)}) copy-start(f32[960,128]{1,0:T(8,128)} %get-tuple-element.21.s_ref) | copy-start | bytes 1474564
  60.6 1.7 %copy-start = (bf16[96,96,128]{2,1,0:T(8,128)(2,1)S(1)}, bf16[96,96,128]{2,1,0:T(8,128)(2,1)}, u32[]{:S(2)}) copy-start(bf16[96,96,128]{2,1,0:T(8,128)(2,1)} %get-tuple-element.18.grad_ref) | copy-start | bytes 7077892
  62.3 1.0 %copy-start.3 = (f32[16,40,128]{2,1,0:T(8,128)S(1)}, f32[16,40,128]{2,1,0:T(8,128)}, u32[]{:S(2)}) copy-start(f32[16,40,128]{2,1,0:T(8,128)} %get-tuple-element.17.in_ref) | copy-start | bytes 983044
  63.3 0.6 copy-start.8
  63.9 4.1 %copy-start.10 = (f32[960,128]{1,0:T(8,128)S(1)}, f32[960,128]{1,0:T(8,128)}, u32[]{:S(2)}) copy-start(f32[960,128]{1,0:T(8,128)} %get-tuple-element.22.t_ref) | copy-start | bytes 1474564
  68.0 3.6 %copy-start.11 = (bf16[96,96,128]{2,1,0:T(8,128)(2,1)S(1)}, bf16[96,96,128]{2,1,0:T(8,128)(2,1)}, u32[]{:S(2)}) copy-start(bf16[96,96,128]{2,1,0:T(8,128)(2,1)} %get-tuple-element.16) | copy-start | bytes 7077892
